TPU v7x, 32 devices: a whole 2x2x4 slice. The times are simulated.
32 devices in a mesh: gx: 4 (over x, core), gy: 8 (over z, y).
Axes of the slice: x: 2, y: 2, z: 4, core: 2. Of those that a mesh axis runs over, the one named last changes fastest.
Arguments:
- incident: float32 [4, 8, 64, 16, 128], P('gx', 'gy'), may hold values from -8 to 8
- positions: float32 [4, 8, 3, 64], P('gx', 'gy'), as said below
- nbr_part: int32 [4, 8, 64, 60], P('gx', 'gy'), may hold values from 0 to 8, as said below
- nbr_slot: int32 [4, 8, 64, 60], P('gx', 'gy'), may hold values from 0 to 63, as said below
- nbr_count: int32 [4, 8, 64], P('gx', 'gy'), may hold values from 1 to 60, as said below
- cluster_id: int32 [4, 8, 64], P('gx', 'gy'), may hold values from 0 to 31, as said below
- mie: float32 [2, 64], replicated, may hold values from -0.45 to 0.45
- to_waves: bfloat16 [2, 64, 128], replicated, may hold values from -0.5 to 0.5
- from_waves: bfloat16 [2, 128, 64], replicated, may hold values from -0.375 to 0.375
- to_cluster: float32 [2, 64, 512], replicated, may hold values from -0.5 to 0.5
- cluster_waves: float32 [2, 512, 961], replicated, may hold values from -0.1875 to 0.1875
- centers: float32 [32, 3], replicated, as said below
Outputs:
- solution: float32 [4, 8, 64, 16, 128], P('gx', 'gy')
- expansions: float32 [32, 16, 1922], P(('gx', 'gy'))
Inputs may be any that keep to these rules, and one draw needn't show every extreme that they name: `positions`: bead (i, j, b) lies in the box 2 i <= x < 2 i + 2, 2 j <= y < 2 j + 2, 0 <= z < 2. `nbr_part`: every entry names a device block that exists on the grid. `nbr_slot`: a slot never names the bead itself. Slots from nbr_count on are padding with arbitrary entries; in every draw some bead has exactly 60 valid slots. `cluster_id`: cluster a * 8 + c is a spatial box; a bead of device (i, j) belongs to cluster min(i + k, 4 - 1) * 8 + min(j + l, 8 - 1) for some k, l in the finite set (0, 1). `centers`: the centre of cluster a * 8 + c lies near the middle of its box.
All inputs are finite; a program needn't handle non-finite values.
Results may differ from a plain program's by a relative error of at most 0.0023.
Values may be sent and summed in bfloat16 or wider, within the bound.
A program may use at most 128 MiB of HBM per device.

v0:
```python
import math

import jax
import jax.numpy as jnp
from jax import lax
from jax.sharding import PartitionSpec as P

WAVE_LAT = 8
WAVE_LON = 16
CLUSTER_LAT = 16
CLUSTER_LON = 32


WAVENUMBER = 3.0
NORM_EPSILON = 1e-06


def extended(block, sides, width):
    for axis, dim in sides:
        count = lax.axis_size(axis)
        forward = [(i, i + 1) for i in range(count - 1)]
        backward = [(target, source) for source, target in forward]
        low = lax.ppermute(
            lax.slice_in_dim(block, block.shape[dim] - width, None, axis=dim), axis, forward
        )
        high = lax.ppermute(lax.slice_in_dim(block, 0, width, axis=dim), axis, backward)
        block = jnp.concatenate([low, block, high], axis=dim)
    return block


def shifted_2(block, axis, distance):
    devices = range(lax.axis_size(axis))
    route = [(i - distance, i) for i in devices if i - distance in devices]
    return lax.ppermute(block, axis, route)


def sphere_grid(cycle_count, cycle_size):
    polar = (jnp.arange(cycle_count, dtype=jnp.float32) + 0.5) * (math.pi / cycle_count)
    cycle_index = jnp.arange(cycle_size, dtype=jnp.float32)
    stagger = 0.5 * (jnp.arange(cycle_count, dtype=jnp.int32) % 2).astype(jnp.float32)
    azimuth = (cycle_index[None, :] + stagger[:, None]) * (2.0 * math.pi / cycle_size)
    height = jnp.cos(polar)[:, None] * jnp.ones_like(azimuth)
    radius = jnp.sin(polar)[:, None]
    return jnp.stack(
        [
            (radius * jnp.cos(azimuth)).reshape(-1),
            (radius * jnp.sin(azimuth)).reshape(-1),
            height.reshape(-1),
        ]
    )


def block_matrix(pair):
    real_part = pair[0]
    imag_part = pair[1]
    top_half = jnp.concatenate([real_part, imag_part], axis=1)
    lower_half = jnp.concatenate([-imag_part, real_part], axis=1)
    return jnp.concatenate([top_half, lower_half], axis=0)


def times_phase(values, cos_part, sin_part):
    half_width = values.shape[-1] // 2
    real_part = values[..., :half_width]
    imag_part = values[..., half_width:]
    return jnp.concatenate(
        [real_part * cos_part - imag_part * sin_part, real_part * sin_part + imag_part * cos_part],
        axis=-1,
    )


def slot_phase(offsets, is_live, directions):
    distance = jnp.sqrt(offsets[0] * offsets[0] + offsets[1] * offsets[1] + offsets[2] * offsets[2])
    scale = jnp.where(is_live, 1.0 / (1.0 + distance), 0.0)
    along_dir = (
        offsets[0][..., None] * directions[0]
        + offsets[1][..., None] * directions[1]
        + offsets[2][..., None] * directions[2]
    )
    phase_angle = WAVENUMBER * along_dir
    return (scale[..., None] * jnp.cos(phase_angle), scale[..., None] * jnp.sin(phase_angle))


def field_sums(pairs):
    local_terms = jnp.stack([jnp.sum(first * second, axis=(0, 2)) for first, second in pairs])
    return lax.psum(local_terms, ("gx", "gy"))


def local(
    incident,
    positions,
    nbr_part,
    nbr_slot,
    nbr_count,
    cluster_id,
    mie,
    to_waves,
    from_waves,
    to_cluster,
    cluster_waves,
    centers,
):
    bead_count = incident.shape[2]
    field_count = incident.shape[3]
    coef_width = incident.shape[4]
    wave_width = 2 * to_waves.shape[2]
    forward_matrix = block_matrix(to_waves)
    back_matrix = block_matrix(from_waves)
    directions = sphere_grid(WAVE_LAT, WAVE_LON)
    pos_ext = extended(positions, (("gx", 0), ("gy", 1)), 1)
    flat_pos = jnp.transpose(pos_ext, (2, 0, 1, 3)).reshape(3, 9 * bead_count)
    flat_index = nbr_part[0, 0] * bead_count + nbr_slot[0, 0]
    counts = nbr_count[0, 0]
    slot_total = flat_index.shape[1]
    slot_numbers = jnp.arange(slot_total, dtype=jnp.int32)
    offsets = positions[0, 0][:, :, None] - flat_pos[:, flat_index]
    phase_cos, phase_sin = slot_phase(offsets, slot_numbers[None, :] < counts[:, None], directions)
    top_count = jnp.max(counts)
    slot_width = slot_total // 4

    def apply_operator(vector):
        vector_low = vector.astype(jnp.bfloat16)
        own_waves = jnp.dot(
            vector_low.reshape(-1, coef_width), forward_matrix, preferred_element_type=jnp.float32
        )
        own_waves = own_waves.astype(jnp.bfloat16).reshape(
            1, 1, bead_count, field_count, wave_width
        )
        wave_ext = extended(own_waves, (("gx", 0), ("gy", 1)), 1)
        wave_rows = wave_ext.reshape(9 * bead_count, field_count, wave_width)
        incoming = jnp.zeros((bead_count, field_count, wave_width), jnp.float32)
        for group_index in range(4):
            first_slot = group_index * slot_width

            def add_group(running, first_slot=first_slot):
                picked = wave_rows[flat_index[:, first_slot : first_slot + slot_width]].astype(
                    jnp.float32
                )
                contribution = times_phase(
                    picked,
                    phase_cos[:, first_slot : first_slot + slot_width, None, :],
                    phase_sin[:, first_slot : first_slot + slot_width, None, :],
                )
                return running + jnp.sum(contribution, axis=1)

            def keep_group(running):
                return running

            incoming = lax.cond(top_count > first_slot, add_group, keep_group, incoming)
        incoming = incoming.astype(jnp.bfloat16)
        back_vals = jnp.dot(
            incoming.reshape(-1, wave_width), back_matrix, preferred_element_type=jnp.float32
        )
        back_vals = back_vals.reshape(bead_count, field_count, coef_width)
        return vector - times_phase(back_vals, mie[0], mie[1])

    source = times_phase(incident[0, 0], mie[0], mie[1])
    beta = jnp.sqrt(field_sums([(source, source)])[0] + NORM_EPSILON)
    basis_one = source / beta[None, :, None]
    image_one = apply_operator(basis_one)
    proj_one = field_sums([(basis_one, image_one)])[0]
    rest_one = image_one - proj_one[None, :, None] * basis_one
    norm_one = jnp.sqrt(field_sums([(rest_one, rest_one)])[0] + NORM_EPSILON)
    basis_two = rest_one / norm_one[None, :, None]
    image_two = apply_operator(basis_two)
    both_proj = field_sums([(basis_one, image_two), (basis_two, image_two)])
    proj_cross = both_proj[0]
    proj_two = both_proj[1]
    rest_two = (
        image_two - proj_cross[None, :, None] * basis_one - proj_two[None, :, None] * basis_two
    )
    rest_square = field_sums([(rest_two, rest_two)])[0] + NORM_EPSILON
    gram_first = proj_one * proj_one + norm_one * norm_one
    gram_cross = proj_one * proj_cross + norm_one * proj_two
    gram_second = proj_cross * proj_cross + proj_two * proj_two + rest_square
    minor_term = proj_one * proj_two - norm_one * proj_cross
    gram_det = minor_term * minor_term + rest_square * gram_first
    weight_one = beta * (gram_second * proj_one - gram_cross * proj_cross) / gram_det
    weight_two = beta * (gram_first * proj_cross - gram_cross * proj_one) / gram_det
    solution = weight_one[None, :, None] * basis_one + weight_two[None, :, None] * basis_two
    cluster_dirs = sphere_grid(CLUSTER_LAT, CLUSTER_LON)
    cluster_forward = block_matrix(to_cluster)
    cluster_back = block_matrix(cluster_waves)
    cluster_total = centers.shape[0]
    sample_width = cluster_forward.shape[1]
    samples = jnp.dot(
        solution.reshape(-1, coef_width), cluster_forward, precision=lax.Precision.HIGHEST
    )
    samples = samples.reshape(bead_count, field_count, sample_width)
    bead_ids = cluster_id[0, 0]
    one_hot = (bead_ids[:, None] == jnp.arange(cluster_total, dtype=jnp.int32)[None, :]).astype(
        jnp.float32
    )
    bead_centre = jnp.dot(one_hot, centers, precision=lax.Precision.HIGHEST)
    cluster_offsets = positions[0, 0] - jnp.transpose(bead_centre)
    along_dir = (
        cluster_offsets[0][:, None] * cluster_dirs[0]
        + cluster_offsets[1][:, None] * cluster_dirs[1]
        + cluster_offsets[2][:, None] * cluster_dirs[2]
    )
    phase_angle = WAVENUMBER * along_dir
    shifted = times_phase(
        samples, jnp.cos(phase_angle)[:, None, :], jnp.sin(phase_angle)[:, None, :]
    )
    shifted_rows = shifted.reshape(bead_count, -1)
    rows_here = cluster_total // lax.axis_size(("gx", "gy"))
    span_y = lax.axis_size("gy")
    place_x = lax.axis_index("gx")
    place_y = lax.axis_index("gy")
    local_code = (bead_ids // span_y - place_x) * 2 + (bead_ids % span_y - place_y)
    local_hot = (local_code[:, None] == jnp.arange(4, dtype=jnp.int32)[None, :]).astype(jnp.float32)
    local_part = jnp.dot(jnp.transpose(local_hot), shifted_rows, precision=lax.Precision.HIGHEST)
    local_exp = jnp.dot(
        local_part.reshape(-1, sample_width), cluster_back, precision=lax.Precision.HIGHEST
    )
    local_exp = local_exp.reshape(4, -1)
    upper_y = jnp.stack([local_exp[1], local_exp[3]])
    from_lower_y = shifted_2(upper_y, "gy", 1)
    section_rows = jnp.stack([local_exp[0], local_exp[2]]) + from_lower_y
    from_lower_x = shifted_2(section_rows[1], "gx", 1)
    own_rows = (section_rows[0] + from_lower_x).reshape(rows_here, -1)
    expansions = own_rows.reshape(rows_here, field_count, cluster_back.shape[1])
    return (solution[None, None], expansions)


def solution(mesh):
    in_specs = (
        P("gx", "gy", None, None, None),
        P("gx", "gy", None, None),
        P("gx", "gy", None, None),
        P("gx", "gy", None, None),
        P("gx", "gy", None),
        P("gx", "gy", None),
        P(),
        P(),
        P(),
        P(),
        P(),
        P(),
    )
    out_specs = (P("gx", "gy", None, None, None), P(("gx", "gy"), None, None))
    return jax.shard_map(local, mesh=mesh, in_specs=in_specs, out_specs=out_specs, check_vma=False)
```

profile of v0, /device:TPU:10, one launch (start us, length us, event | category | flops | bytes accessed | tf_op | source)
XLA Modules:
  0.0 801.2 jit_solution(14559577419394638775)
XLA Ops:
  4.7 41.3 %psum.35 = f32[1,16]{1,0:T(1,128)S(1)} all-reduce(f32[1,16]{1,0:T(1,128)S(1)} %bitcast.198), channel_id=1, replica_groups=mesh['gx'=4,'gy'=8] {'gx','gy'}, use_global_device_ids=true, to_apply=%region_1.2 | all-reduce | flops 16 | bytes 128 | tf_op jit(solution)/shard_map/psum | solution.py:85
  84.1 50.6 %collective-permute-done.6 = f32[3,1,3,64]{3,1,2,0:T(1,128)S(1)} collective-permute-done((f32[3,1,3,64]{3,1,2,0:T(1,128)S(1)}, f32[3,1,3,64]{3,1,2,0:T(1,128)S(1)}, u32[]{:S(2)}, u32[]{:S(2)}) %collective-permute-start.6) | collective-permute-done | bytes 2336 | tf_op jit(solution)/shard_map/ppermute | solution.py:23
  137.7 7.9 gather_fusion.8
  148.1 15.2 %sine_multiply_fusion = (f32[64,60,128]{2,1,0:T(8,128)S(1)}, f32[64,60,128]{2,1,0:T(8,128)}) fusion(f32[128]{0:T(128)S(1)} %mul.944, f32[64,60]{1,0:T(8,128)S(1)} %get-tuple-element.201, f32[128]{0:T(128)S(1)} %mul.939, f32[64,60]{1,0:T(8,128)S(1)} %get-tuple-element.202, f32[128]{0:T(128)S(1)} %mul.934, f32[64,60]{1,0:T(8,128)S(1)} %get-tuple-element.200, ...), kind=kLoop, calls=%fused_computation.60 | loop fusion | flops 3932160 | bytes 3995136 | tf_op jit(solution)/shard_map/mul | solution.py:80
  167.4 41.0 %conditional.8 = (f32[64,16,256]{2,1,0:T(8,128)S(1)}) conditional(s32[]{:T(128)} %convert_element_type.95, () %tuple.76, (s32[64,60]{1,0:T(8,128)S(1)}, bf16[576,16,256]{2,1,0:T(8,128)(2,1)}, f32[64,60,128]{2,1,0:T(8,128)}, f32[64,60,128]{2,1,0:T(8,128)S(1)}) %tuple.144), branch_computations={%region_3.4_spmd, %region_4.6_spmd} | conditional | flops 23334720 | bytes 90532360 | solution.py:148
  167.6 11.8 %gather_fusion = bf16[960,16,256]{2,1,0:T(8,128)(2,1)} fusion(bf16[576,16,256]{2,1,0:T(8,128)(2,1)} %get-tuple-element.118, s32[1024]{0:T(1024)S(1)} %pad_clamp_fusion), kind=kCustom, calls=%fused_computation | custom fusion | bytes 15732480 | tf_op jit(solution)/shard_map/cond/branch_1_fun/gather | solution.py:135
  179.4 10.9 %convert = f32[64,15,16,256]{3,2,1,0:T(8,128)} convert(bf16[64,15,16,256]{3,2,1,0:T(8,128)(2,1)} %bitcast.163) | non-fusion elementwise | flops 3932160 | bytes 23592960 | tf_op jit(solution)/shard_map/cond/branch_1_fun/convert_element_type | solution.py:135
  191.4 10.2 %multiply_subtract_fusion = (f32[64,15,16,128]{3,2,1,0:T(8,128)}, f32[64,15,16,128]{3,2,1,0:T(8,128)}) fusion(f32[64,15,16,256]{3,2,1,0:T(8,128)} %convert, f32[64,15,128]{2,1,0:T(8,128)S(1)} %slice.166, f32[64,15,128]{2,1,0:T(8,128)S(1)} %slice.164), kind=kLoop, calls=%fused_computation.11 | loop fusion | flops 11796480 | bytes 32440320 | tf_op jit(solution)/shard_map/cond/branch_1_fun/sub | solution.py:66
  201.6 6.9 maximum_reduce_fusion
  208.5 41.9 %conditional.9 = (f32[64,16,256]{2,1,0:T(8,128)S(1)}) conditional(s32[]{:T(128)} %convert_element_type.94, f32[64,16,256]{2,1,0:T(8,128)S(1)} %get-tuple-element.228, (s32[64,60]{1,0:T(8,128)S(1)}, bf16[576,16,256]{2,1,0:T(8,128)(2,1)}, f32[64,60,128]{2,1,0:T(8,128)}, f32[64,60,128]{2,1,0:T(8,128)S(1)}, f32[64,16,256]{2,1,0:T(8,128)S(1)}) %tuple.145), branch_computations={%region_6.7_spmd, %region_7.9_spmd} | conditional | flops 23596864 | bytes 93678088 | solution.py:148
  209.0 11.8 %gather_fusion.1 = bf16[960,16,256]{2,1,0:T(8,128)(2,1)} fusion(bf16[576,16,256]{2,1,0:T(8,128)(2,1)} %get-tuple-element.123, s32[1024]{0:T(1024)S(1)} %pad_clamp_fusion.1), kind=kCustom, calls=%fused_computation.1 | custom fusion | bytes 15732480 | tf_op jit(solution)/shard_map/cond/branch_1_fun/gather | solution.py:135
  220.8 10.9 %convert.1 = f32[64,15,16,256]{3,2,1,0:T(8,128)} convert(bf16[64,15,16,256]{3,2,1,0:T(8,128)(2,1)} %bitcast.164) | non-fusion elementwise | flops 3932160 | bytes 23592960 | tf_op jit(solution)/shard_map/cond/branch_1_fun/convert_element_type | solution.py:135
  233.0 10.2 %multiply_subtract_fusion.1 = (f32[64,15,16,128]{3,2,1,0:T(8,128)}, f32[64,15,16,128]{3,2,1,0:T(8,128)}) fusion(f32[64,15,16,256]{3,2,1,0:T(8,128)} %convert.1, f32[64,15,128]{2,1,0:T(8,128)S(1)} %slice.171, f32[64,15,128]{2,1,0:T(8,128)S(1)} %slice.169), kind=kLoop, calls=%fused_computation.16 | loop fusion | flops 11796480 | bytes 32440320 | tf_op jit(solution)/shard_map/cond/branch_1_fun/sub | solution.py:66
  243.2 6.9 maximum_reduce_fusion.1
  254.0 121.7 %psum.36 = f32[16]{0:T(128)S(1)} all-reduce(f32[16]{0:T(128)S(1)} %get-tuple-element.164), channel_id=1, replica_groups=mesh['gx'=4,'gy'=8] {'gx','gy'}, use_global_device_ids=true, to_apply=%region_16.17 | all-reduce | flops 16 | bytes 128 | tf_op jit(solution)/shard_map/psum | solution.py:85
  377.9 41.5 %psum.37 = f32[1,16]{1,0:T(1,128)S(1)} all-reduce(f32[1,16]{1,0:T(1,128)S(1)} %bitcast.200), channel_id=1, replica_groups=mesh['gx'=4,'gy'=8] {'gx','gy'}, use_global_device_ids=true, to_apply=%region_18.19 | all-reduce | flops 16 | bytes 128 | tf_op jit(solution)/shard_map/psum | solution.py:85
  447.4 6.7 fusion.62
  458.1 48.2 %collective-permute-done.10 = bf16[3,1,64,16,256]{4,3,2,1,0:T(8,128)(2,1)S(1)} collective-permute-done((bf16[3,1,64,16,256]{4,3,2,1,0:T(8,128)(2,1)S(1)}, bf16[3,1,64,16,256]{4,3,2,1,0:T(8,128)(2,1)S(1)}, u32[]{:S(2)}, u32[]{:S(2)}) %collective-permute-start.10) | collective-permute-done | bytes 1572896 | tf_op jit(solution)/shard_map/ppermute | solution.py:23
  513.0 41.0 %conditional.12 = (f32[64,16,256]{2,1,0:T(8,128)S(1)}) conditional(s32[]{:T(128)} %convert_element_type.95, () %tuple.81, (s32[64,60]{1,0:T(8,128)S(1)}, bf16[576,16,256]{2,1,0:T(8,128)(2,1)}, f32[64,60,128]{2,1,0:T(8,128)}, f32[64,60,128]{2,1,0:T(8,128)S(1)}) %tuple.140), branch_computations={%region_19.20_spmd, %region_20.22_spmd} | conditional | flops 23334720 | bytes 90532360 | solution.py:148
  513.2 11.8 %gather_fusion.4 = bf16[960,16,256]{2,1,0:T(8,128)(2,1)} fusion(bf16[576,16,256]{2,1,0:T(8,128)(2,1)} %get-tuple-element.137, s32[1024]{0:T(1024)S(1)} %pad_clamp_fusion.4), kind=kCustom, calls=%fused_computation.4 | custom fusion | bytes 15732480 | tf_op jit(solution)/shard_map/cond/branch_1_fun/gather | solution.py:135
  524.9 10.9 %convert.4 = f32[64,15,16,256]{3,2,1,0:T(8,128)} convert(bf16[64,15,16,256]{3,2,1,0:T(8,128)(2,1)} %bitcast.167) | non-fusion elementwise | flops 3932160 | bytes 23592960 | tf_op jit(solution)/shard_map/cond/branch_1_fun/convert_element_type | solution.py:135
  537.0 10.2 %multiply_subtract_fusion.4 = (f32[64,15,16,128]{3,2,1,0:T(8,128)}, f32[64,15,16,128]{3,2,1,0:T(8,128)}) fusion(f32[64,15,16,256]{3,2,1,0:T(8,128)} %convert.4, f32[64,15,128]{2,1,0:T(8,128)S(1)} %slice.186, f32[64,15,128]{2,1,0:T(8,128)S(1)} %slice.184), kind=kLoop, calls=%fused_computation.31 | loop fusion | flops 11796480 | bytes 32440320 | tf_op jit(solution)/shard_map/cond/branch_1_fun/sub | solution.py:66
  547.2 6.9 maximum_reduce_fusion.4
  554.1 41.8 %conditional.13 = (f32[64,16,256]{2,1,0:T(8,128)S(1)}) conditional(s32[]{:T(128)} %convert_element_type.94, f32[64,16,256]{2,1,0:T(8,128)S(1)} %get-tuple-element.232, (s32[64,60]{1,0:T(8,128)S(1)}, bf16[576,16,256]{2,1,0:T(8,128)(2,1)}, f32[64,60,128]{2,1,0:T(8,128)}, f32[64,60,128]{2,1,0:T(8,128)S(1)}, f32[64,16,256]{2,1,0:T(8,128)S(1)}) %tuple.141), branch_computations={%region_22.23_spmd, %region_23.25_spmd} | conditional | flops 23596864 | bytes 93678088 | solution.py:148
  554.5 11.8 %gather_fusion.5 = bf16[960,16,256]{2,1,0:T(8,128)(2,1)} fusion(bf16[576,16,256]{2,1,0:T(8,128)(2,1)} %get-tuple-element.142, s32[1024]{0:T(1024)S(1)} %pad_clamp_fusion.5), kind=kCustom, calls=%fused_computation.5 | custom fusion | bytes 15732480 | tf_op jit(solution)/shard_map/cond/branch_1_fun/gather | solution.py:135
  566.3 10.9 %convert.5 = f32[64,15,16,256]{3,2,1,0:T(8,128)} convert(bf16[64,15,16,256]{3,2,1,0:T(8,128)(2,1)} %bitcast.168) | non-fusion elementwise | flops 3932160 | bytes 23592960 | tf_op jit(solution)/shard_map/cond/branch_1_fun/convert_element_type | solution.py:135
  578.5 10.2 %multiply_subtract_fusion.5 = (f32[64,15,16,128]{3,2,1,0:T(8,128)}, f32[64,15,16,128]{3,2,1,0:T(8,128)}) fusion(f32[64,15,16,256]{3,2,1,0:T(8,128)} %convert.5, f32[64,15,128]{2,1,0:T(8,128)S(1)} %slice.191, f32[64,15,128]{2,1,0:T(8,128)S(1)} %slice.189), kind=kLoop, calls=%fused_computation.36 | loop fusion | flops 11796480 | bytes 32440320 | tf_op jit(solution)/shard_map/cond/branch_1_fun/sub | solution.py:66
  588.7 6.9 maximum_reduce_fusion.5
  598.5 121.6 %psum.38 = f32[2,16]{1,0:T(2,128)S(1)} all-reduce(f32[2,16]{1,0:T(2,128)S(1)} %pad_maximum_fusion.10), channel_id=1, replica_groups=mesh['gx'=4,'gy'=8] {'gx','gy'}, use_global_device_ids=true, to_apply=%region_33.34 | all-reduce | flops 32 | bytes 256 | tf_op jit(solution)/shard_map/psum | solution.py:85
  721.7 42.0 %psum.39 = f32[1,16]{1,0:T(1,128)S(1)} all-reduce(f32[1,16]{1,0:T(1,128)S(1)} %bitcast.197), channel_id=1, replica_groups=mesh['gx'=4,'gy'=8] {'gx','gy'}, use_global_device_ids=true, to_apply=%region_35.36 | all-reduce | flops 16 | bytes 128 | tf_op jit(solution)/shard_map/psum | solution.py:85
  772.8 10.5 %fusion.1 = f32[64,1922]{1,0:T(8,128)S(1)} fusion(f32[64,1024]{1,0:T(8,128)S(1)} %reshape.755, f32[512,961]{0,1:T(8,128)} %get-tuple-element.227, f32[512,961]{0,1:T(8,128)} %fusion.61, f32[512,961]{0,1:T(8,128)} %get-tuple-element.226), kind=kOutput, calls=%fused_computation.51 | convolution fusion | flops 1517426688 | bytes 6658560 | tf_op jit(solution)/shard_map/dot_general | solution.py:212
  786.5 6.5 collective-permute-done.12
  (226 shorter events, 123.3 us)
Async XLA Ops:
  2.9 248.4 %copy-start.28 = (f32[64]{0:T(128)}, f32[64]{0:T(128)S(1)}, u32[]{:S(2)}) copy-start(f32[64]{0:T(128)S(1)} %get-tuple-element.220) | copy-start | bytes 772
  2.9 248.4 %copy-start.30 = (f32[64]{0:T(128)}, f32[64]{0:T(128)S(1)}, u32[]{:S(2)}) copy-start(f32[64]{0:T(128)S(1)} %get-tuple-element.221) | copy-start | bytes 772
  4.4 158.9 %copy-start.4 = (f32[64,16,64]{2,1,0:T(8,128)}, f32[64,16,64]{2,1,0:T(8,128)S(1)}, u32[]{:S(2)}) copy-start(f32[64,16,64]{2,1,0:T(8,128)S(1)} %get-tuple-element.190) | copy-start | bytes 786436
  46.0 205.6 %copy-start.33 = (f32[16]{0:T(128)}, f32[16]{0:T(128)S(1)}, u32[]{:S(2)}) copy-start(f32[16]{0:T(128)S(1)} %sqrt_bitcast_fusion.1) | copy-start | bytes 196
  46.6 17.3 %collective-permute-start = (bf16[1,1,64,16,256]{4,3,2,1,0:T(8,128)(2,1)S(1)}, bf16[1,1,64,16,256]{4,3,2,1,0:T(8,128)(2,1)S(1)}, u32[]{:S(2)}, u32[]{:S(2)}) collective-permute-start(bf16[1,1,64,16,256]{4,3,2,1,0:T(8,128)(2,1)S(1)} %bitcast.184), channel_id=1, source_target_pairs={{0,8},{8,16},{16,24},{1,9},{9,17},{17,25},{2,10},{10,18},{18,26},{... | collective-permute-start | bytes 1572872 | tf_op jit(solution)/shard_map/ppermute | solution.py:23
  48.6 15.4 %collective-permute-start.1 = (bf16[1,1,64,16,256]{4,3,2,1,0:T(8,128)(2,1)S(1)}, bf16[1,1,64,16,256]{4,3,2,1,0:T(8,128)(2,1)S(1)}, u32[]{:S(2)}, u32[]{:S(2)}) collective-permute-start(bf16[1,1,64,16,256]{4,3,2,1,0:T(8,128)(2,1)S(1)} %bitcast.185), channel_id=1, source_target_pairs={{8,0},{16,8},{24,16},{9,1},{17,9},{25,17},{10,2},{18,10},{26,18},{... | collective-permute-start | bytes 1572872 | tf_op jit(solution)/shard_map/ppermute | solution.py:26
  52.2 20.0 %collective-permute-start.4 = (f32[1,1,3,64]{3,1,2,0:T(1,128)}, f32[1,1,3,64]{3,1,2,0:T(1,128)S(1)}, u32[]{:S(2)}, u32[]{:S(2)}) collective-permute-start(f32[1,1,3,64]{3,1,2,0:T(1,128)} %param.29), channel_id=1, source_target_pairs={{0,8},{8,16},{16,24},{1,9},{9,17},{17,25},{2,10},{10,18},{18,26},{... | collective-permute-start | bytes 2312 | tf_op jit(solution)/shard_map/ppermute | solution.py:23
  54.1 18.1 %collective-permute-start.5 = (f32[1,1,3,64]{3,1,2,0:T(1,128)}, f32[1,1,3,64]{3,1,2,0:T(1,128)S(1)}, u32[]{:S(2)}, u32[]{:S(2)}) collective-permute-start(f32[1,1,3,64]{3,1,2,0:T(1,128)} %param.29), channel_id=1, source_target_pairs={{8,0},{16,8},{24,16},{9,1},{17,9},{25,17},{10,2},{18,10},{26,18},{... | collective-permute-start | bytes 2312 | tf_op jit(solution)/shard_map/ppermute | solution.py:26
  65.5 97.8 %collective-permute-start.2 = (bf16[3,1,64,16,256]{4,3,2,1,0:T(8,128)(2,1)}, bf16[3,1,64,16,256]{4,3,2,1,0:T(8,128)(2,1)}, u32[]{:S(2)}, u32[]{:S(2)}) collective-permute-start(bf16[3,1,64,16,256]{4,3,2,1,0:T(8,128)(2,1)} %pad_maximum_fusion.6), channel_id=1, source_target_pairs={{0,1},{1,2},{2,3},{3,4},{4,5},{5,6},{6,7},{8,9},{9,10},{10,11},{11... | collective-permute-start | bytes 4718600 | tf_op jit(solution)/shard_map/ppermute | solution.py:23
  67.9 95.4 %collective-permute-start.3 = (bf16[3,1,64,16,256]{4,3,2,1,0:T(8,128)(2,1)}, bf16[3,1,64,16,256]{4,3,2,1,0:T(8,128)(2,1)}, u32[]{:S(2)}, u32[]{:S(2)}) collective-permute-start(bf16[3,1,64,16,256]{4,3,2,1,0:T(8,128)(2,1)} %pad_maximum_fusion.6), channel_id=1, source_target_pairs={{1,0},{2,1},{3,2},{4,3},{5,4},{6,5},{7,6},{9,8},{10,9},{11,10},{12... | collective-permute-start | bytes 4718600 | tf_op jit(solution)/shard_map/ppermute | solution.py:26
  72.3 62.3 %collective-permute-start.6 = (f32[3,1,3,64]{3,1,2,0:T(1,128)S(1)}, f32[3,1,3,64]{3,1,2,0:T(1,128)S(1)}, u32[]{:S(2)}, u32[]{:S(2)}) collective-permute-start(f32[3,1,3,64]{3,1,2,0:T(1,128)S(1)} %constant_dynamic-update-slice_fusion), channel_id=1, source_target_pairs={{0,1},{1,2},{2,3},{3,4},{4,5},{5,6},{6,7},{8,9},{9,10},{10,11},{11... | collective-permute-start | bytes 6920 | tf_op jit(solution)/shard_map/ppermute | solution.py:23
  74.2 63.3 %collective-permute-start.7 = (f32[3,1,3,64]{3,1,2,0:T(1,128)S(1)}, f32[3,1,3,64]{3,1,2,0:T(1,128)S(1)}, u32[]{:S(2)}, u32[]{:S(2)}) collective-permute-start(f32[3,1,3,64]{3,1,2,0:T(1,128)S(1)} %constant_dynamic-update-slice_fusion), channel_id=1, source_target_pairs={{1,0},{2,1},{3,2},{4,3},{5,4},{6,5},{7,6},{9,8},{10,9},{11,10},{12... | collective-permute-start | bytes 6920 | tf_op jit(solution)/shard_map/ppermute | solution.py:26
  250.9 181.9 %copy-start.25 = (f32[512]{0:T(512)S(1)}, f32[512]{0:T(512)}, u32[]{:S(2)}) copy-start(f32[512]{0:T(512)} %mul.1011) | copy-start | bytes 6148
  250.9 183.9 %copy-start.16 = (f32[2,64,512]{2,1,0:T(8,128)S(1)}, f32[2,64,512]{2,1,0:T(8,128)}, u32[]{:S(2)}) copy-start(f32[2,64,512]{2,1,0:T(8,128)} %param.37) | copy-start | bytes 786436
  251.6 202.6 %copy-start.8 = (f32[64,16,64]{2,1,0:T(8,128)}, f32[64,16,64]{2,1,0:T(8,128)S(1)}, u32[]{:S(2)}) copy-start(f32[64,16,64]{2,1,0:T(8,128)S(1)} %get-tuple-element.188) | copy-start | bytes 786436
  254.0 200.1 %copy-start.2 = (f32[64,16,128]{2,1,0:T(8,128)}, f32[64,16,128]{2,1,0:T(8,128)S(1)}, u32[]{:S(2)}) copy-start(f32[64,16,128]{2,1,0:T(8,128)S(1)} %get-tuple-element.165) | copy-start | bytes 1572868
  426.4 10.8 %collective-permute-start.8 = (bf16[1,1,64,16,256]{4,3,2,1,0:T(8,128)(2,1)}, bf16[1,1,64,16,256]{4,3,2,1,0:T(8,128)(2,1)}, u32[]{:S(2)}, u32[]{:S(2)}) collective-permute-start(bf16[1,1,64,16,256]{4,3,2,1,0:T(8,128)(2,1)} %bitcast.43), channel_id=1, source_target_pairs={{0,8},{8,16},{16,24},{1,9},{9,17},{17,25},{2,10},{10,18},{18,26},{... | collective-permute-start | bytes 1572872 | tf_op jit(solution)/shard_map/ppermute | solution.py:23
  428.3 10.6 %collective-permute-start.9 = (bf16[1,1,64,16,256]{4,3,2,1,0:T(8,128)(2,1)}, bf16[1,1,64,16,256]{4,3,2,1,0:T(8,128)(2,1)}, u32[]{:S(2)}, u32[]{:S(2)}) collective-permute-start(bf16[1,1,64,16,256]{4,3,2,1,0:T(8,128)(2,1)} %bitcast.43), channel_id=1, source_target_pairs={{8,0},{16,8},{24,16},{9,1},{17,9},{25,17},{10,2},{18,10},{26,18},{... | collective-permute-start | bytes 1572872 | tf_op jit(solution)/shard_map/ppermute | solution.py:26
  440.5 65.8 %collective-permute-start.10 = (bf16[3,1,64,16,256]{4,3,2,1,0:T(8,128)(2,1)S(1)}, bf16[3,1,64,16,256]{4,3,2,1,0:T(8,128)(2,1)S(1)}, u32[]{:S(2)}, u32[]{:S(2)}) collective-permute-start(bf16[3,1,64,16,256]{4,3,2,1,0:T(8,128)(2,1)S(1)} %pad_maximum_fusion.7), channel_id=1, source_target_pairs={{0,1},{1,2},{2,3},{3,4},{4,5},{5,6},{6,7},{8,9},{9,10},{10,11},{11... | collective-permute-start | bytes 4718600 | tf_op jit(solution)/shard_map/ppermute | solution.py:23
  442.6 66.8 %collective-permute-start.11 = (bf16[3,1,64,16,256]{4,3,2,1,0:T(8,128)(2,1)S(1)}, bf16[3,1,64,16,256]{4,3,2,1,0:T(8,128)(2,1)S(1)}, u32[]{:S(2)}, u32[]{:S(2)}) collective-permute-start(bf16[3,1,64,16,256]{4,3,2,1,0:T(8,128)(2,1)S(1)} %pad_maximum_fusion.7), channel_id=1, source_target_pairs={{1,0},{2,1},{3,2},{4,3},{5,4},{6,5},{7,6},{9,8},{10,9},{11,10},{12... | collective-permute-start | bytes 4718600 | tf_op jit(solution)/shard_map/ppermute | solution.py:26
  596.2 167.5 %copy-start.27 = (f32[16]{0:T(128)S(1)}, f32[16]{0:T(128)}, u32[]{:S(2)}) copy-start(f32[16]{0:T(128)} %copy-done.26) | copy-start | bytes 196
  596.2 167.5 %copy-start.39 = (f32[1,16]{1,0:T(1,128)S(1)}, f32[1,16]{1,0:T(1,128)}, u32[]{:S(2)}) copy-start(f32[1,16]{1,0:T(1,128)} %copy-done.38) | copy-start | bytes 196
  596.2 167.5 %copy-start.41 = (f32[1,16]{1,0:T(1,128)S(1)}, f32[1,16]{1,0:T(1,128)}, u32[]{:S(2)}) copy-start(f32[1,16]{1,0:T(1,128)} %copy-done.40) | copy-start | bytes 196
  596.2 167.5 %copy-start.3 = (f32[64,16,128]{2,1,0:T(8,128)S(1)}, f32[64,16,128]{2,1,0:T(8,128)}, u32[]{:S(2)}) copy-start(f32[64,16,128]{2,1,0:T(8,128)} %copy-done.2) | copy-start | bytes 1572868
  596.2 167.5 %copy-start.12 = (f32[64,16,128]{2,1,0:T(8,128)S(1)}, f32[64,16,128]{2,1,0:T(8,128)}, u32[]{:S(2)}) copy-start(f32[64,16,128]{2,1,0:T(8,128)} %get-tuple-element.163) | copy-start | bytes 1572868
  596.2 167.5 %copy-start.19 = (f32[64,512]{1,0:T(8,128)S(1)}, f32[64,512]{1,0:T(8,128)}, u32[]{:S(2)}) copy-start(f32[64,512]{1,0:T(8,128)} %fusion.60) | copy-start | bytes 393220
  596.3 167.5 %copy-start.20 = (f32[64,512]{1,0:T(8,128)S(1)}, f32[64,512]{1,0:T(8,128)}, u32[]{:S(2)}) copy-start(f32[64,512]{1,0:T(8,128)} %get-tuple-element.196) | copy-start | bytes 393220
  596.3 167.5 %copy-start.21 = (f32[64,512]{1,0:T(8,128)S(1)}, f32[64,512]{1,0:T(8,128)}, u32[]{:S(2)}) copy-start(f32[64,512]{1,0:T(8,128)} %get-tuple-element.197) | copy-start | bytes 393220
  596.3 171.0 %copy-start.17 = (f32[64,512]{1,0:T(8,128)S(1)}, f32[64,512]{1,0:T(8,128)}, u32[]{:S(2)}) copy-start(f32[64,512]{1,0:T(8,128)} %get-tuple-element.207) | copy-start | bytes 393220
  596.3 171.0 %copy-start.18 = (f32[64,512]{1,0:T(8,128)S(1)}, f32[64,512]{1,0:T(8,128)}, u32[]{:S(2)}) copy-start(f32[64,512]{1,0:T(8,128)} %get-tuple-element.208) | copy-start | bytes 393220
  784.1 9.0 %collective-permute-start.12 = (f32[2,30752]{1,0:T(2,128)S(1)}, f32[2,30752]{1,0:T(2,128)S(1)}, u32[]{:S(2)}, u32[]{:S(2)}) collective-permute-start(f32[2,30752]{1,0:T(2,128)S(1)} %pad_maximum_fusion.9), channel_id=1, source_target_pairs={{0,1},{1,2},{2,3},{3,4},{4,5},{5,6},{6,7},{8,9},{9,10},{10,11},{11... | collective-permute-start | bytes 738056 | tf_op jit(solution)/shard_map/ppermute | solution.py:34
  794.0 6.2 collective-permute-start.13
  (24 other events, 1021.3 us)
where the time goes:
time: 811 us; the launch traced here: 801 us
  blocking collectives  368 us (45%)
  other arithmetic  158 us (19%)
  waiting for transfers between devices  118 us (15%)
  local copies, waits for them, and re-layouts  89.7 us (11%)
  starting transfers between devices  41 us (5%)
  matrix products  20.6 us (3%)
    psum x5, blocking collectives, field_sums(): return lax.psum(local_terms, ('gx', 'gy'))  368 us
    ppermute x6, waiting for transfers between devices, extended(): lax.ppermute(lax.slice_in_dim(block, block.shape[dim] - width, None, axis...  101 us
    gather x4, local copies, waits for them, and re-layouts, add_group(): wave_rows[flat_index[:, first_slot:first_slot + slot_width]]  47 us
    convert_element_type x4, other arithmetic, add_group(): wave_rows[flat_index[:, first_slot:first_slot + slot_width]]  43.8 us
    sub x8, other arithmetic, times_phase(): real_part * cos_part - imag_part * sin_part  43.4 us
    reduce_sum x4, other arithmetic, add_group(): return running + jnp.sum(contribution, axis=1)  27.5 us
    ppermute x6, starting transfers between devices, extended(): lax.ppermute(lax.slice_in_dim(block, 0, width, axis=dim), axis, backward)  24.9 us
  transfers between devices with their start and end apart: 14, of which 8 were waited for; matrix products, arithmetic and copies ran while one was open for 6% of the time, Pallas kernels for 0%

commit v1 on v0

v1 whole, which is shorter than its diff:
```python
import math

import jax
import jax.numpy as jnp
from jax import lax
from jax.sharding import PartitionSpec as P

WAVE_LAT = 8
WAVE_LON = 16
CLUSTER_LAT = 16
CLUSTER_LON = 32
WAVENUMBER = 3.0
EPS = 1e-06
HI = lax.Precision.HIGHEST


def shift(block, axis, distance):
    count = lax.axis_size(axis)
    route = [(i - distance, i) for i in range(count) if 0 <= i - distance < count]
    return lax.ppermute(block, axis, route)


def extended(block):
    column = jnp.stack([shift(block, "gy", 1), block, shift(block, "gy", -1)])
    return jnp.stack([shift(column, "gx", 1), column, shift(column, "gx", -1)])


def sphere_grid(cycle_count, cycle_size):
    polar = (jnp.arange(cycle_count, dtype=jnp.float32) + 0.5) * (math.pi / cycle_count)
    cycle_index = jnp.arange(cycle_size, dtype=jnp.float32)
    stagger = 0.5 * (jnp.arange(cycle_count, dtype=jnp.int32) % 2).astype(jnp.float32)
    azimuth = (cycle_index[None, :] + stagger[:, None]) * (2.0 * math.pi / cycle_size)
    height = jnp.cos(polar)[:, None] * jnp.ones_like(azimuth)
    radius = jnp.sin(polar)[:, None]
    return jnp.stack(
        [
            (radius * jnp.cos(azimuth)).reshape(-1),
            (radius * jnp.sin(azimuth)).reshape(-1),
            height.reshape(-1),
        ]
    )


def block_matrix(pair):
    top_half = jnp.concatenate([pair[0], pair[1]], axis=1)
    lower_half = jnp.concatenate([-pair[1], pair[0]], axis=1)
    return jnp.concatenate([top_half, lower_half], axis=0)


def times_phase(values, cos_part, sin_part):
    half_width = values.shape[-1] // 2
    real_part = values[..., :half_width]
    imag_part = values[..., half_width:]
    return jnp.concatenate(
        [real_part * cos_part - imag_part * sin_part, real_part * sin_part + imag_part * cos_part],
        axis=-1,
    )


def angles(pos, dirs):
    along = pos[0][:, None] * dirs[0] + pos[1][:, None] * dirs[1] + pos[2][:, None] * dirs[2]
    return WAVENUMBER * along


def weights(gram):
    ss, st, tt, su, tu, uu = [gram[k] for k in range(6)]
    beta2 = ss + EPS
    beta = jnp.sqrt(beta2)
    h11 = (ss - st) / beta2
    c = (st + EPS) / beta2
    rest = jnp.maximum((c * c * ss - 2.0 * c * st + tt) / beta2, 0.0)
    h21 = jnp.sqrt(rest + EPS)
    r = -1.0 / (beta * h21)
    p = -c * r
    h12 = (p * ss + (r - p) * st - r * su) / beta
    h22 = p * (p * ss + (r - p) * st - r * su) + r * (p * st + (r - p) * tt - r * tu)
    a = p - h12 / beta - h22 * p
    b = r - p - h22 * r
    g = -r
    q = a * a * ss + b * b * tt + g * g * uu + 2.0 * (a * b * st + a * g * su + b * g * tu)
    q = jnp.maximum(q, 0.0) + EPS
    gram_first = h11 * h11 + h21 * h21
    gram_cross = h11 * h12 + h21 * h22
    gram_second = h12 * h12 + h22 * h22 + q
    minor = h11 * h22 - h21 * h12
    det = minor * minor + q * gram_first
    y1 = beta * (gram_second * h11 - gram_cross * h12) / det
    y2 = beta * (gram_first * h12 - gram_cross * h11) / det
    return y1 / beta + y2 * p, y2 * r


def local(
    incident,
    positions,
    nbr_part,
    nbr_slot,
    nbr_count,
    cluster_id,
    mie,
    to_waves,
    from_waves,
    to_cluster,
    cluster_waves,
    centers,
):
    bead_count = incident.shape[2]
    field_count = incident.shape[3]
    coef_width = incident.shape[4]
    wave_count = to_waves.shape[2]
    forward_matrix = block_matrix(to_waves)
    back_matrix = block_matrix(from_waves)
    source = times_phase(jnp.transpose(incident[0, 0], (1, 0, 2)), mie[0], mie[1])
    own_pos = positions[0, 0]
    all_pos = jnp.transpose(extended(own_pos), (2, 0, 1, 3)).reshape(3, 9 * bead_count)
    flat_index = nbr_part[0, 0] * bead_count + nbr_slot[0, 0]
    slots = jnp.arange(flat_index.shape[1], dtype=jnp.int32)
    flat_index = jnp.where(slots[None, :] < nbr_count[0, 0][:, None], flat_index, -1)
    rows = jnp.arange(9 * bead_count, dtype=jnp.int32)
    times = jnp.sum((flat_index[:, :, None] == rows).astype(jnp.float32), axis=1)
    diff = own_pos[:, :, None] - all_pos[:, None, :]
    dist = jnp.sqrt(diff[0] * diff[0] + diff[1] * diff[1] + diff[2] * diff[2])
    weight = times / (1.0 + dist)
    weight_hi = weight.astype(jnp.bfloat16)
    weight_lo = (weight - weight_hi.astype(jnp.float32)).astype(jnp.bfloat16)
    weight_pair = jnp.concatenate([weight_hi, weight_lo], axis=0)
    dirs = sphere_grid(WAVE_LAT, WAVE_LON)
    own_angle = angles(own_pos, dirs)
    own_cos, own_sin = jnp.cos(own_angle), jnp.sin(own_angle)
    all_angle = angles(all_pos, dirs)
    all_cos, all_sin = jnp.cos(all_angle), jnp.sin(all_angle)

    def scatter(vector):
        low = vector.astype(jnp.bfloat16)
        blocks = extended(low)
        blocks = jnp.transpose(blocks, (2, 0, 1, 3, 4)).reshape(
            field_count, 9 * bead_count, coef_width
        )
        samples = jnp.einsum(
            "fnc,cq->fnq", blocks, forward_matrix, preferred_element_type=jnp.float32
        )
        turned = times_phase(samples, all_cos, -all_sin).astype(jnp.bfloat16)
        both = jnp.einsum("bn,fnq->fbq", weight_pair, turned, preferred_element_type=jnp.float32)
        incoming = both[:, :bead_count] + both[:, bead_count:]
        incoming = times_phase(incoming, own_cos, own_sin).astype(jnp.bfloat16)
        back = jnp.einsum(
            "fbq,qc->fbc", incoming, back_matrix, preferred_element_type=jnp.float32
        )
        return times_phase(back, mie[0], mie[1])

    once = scatter(source)
    twice = scatter(once)
    pairs = (
        (source, source),
        (source, once),
        (once, once),
        (source, twice),
        (once, twice),
        (twice, twice),
    )
    gram = jnp.stack([jnp.sum(x * y, axis=(1, 2)) for x, y in pairs])
    gram = lax.psum(gram, ("gx", "gy"))
    w_source, w_once = weights(gram)
    answer = w_source[:, None, None] * source + w_once[:, None, None] * once

    cluster_dirs = sphere_grid(CLUSTER_LAT, CLUSTER_LON)
    samples = jnp.einsum("fbc,cq->fbq", answer, block_matrix(to_cluster), precision=HI)
    bead_ids = cluster_id[0, 0]
    cluster_total = centers.shape[0]
    one_hot = (bead_ids[:, None] == jnp.arange(cluster_total, dtype=jnp.int32)[None, :]).astype(
        jnp.float32
    )
    bead_centre = jnp.dot(one_hot, centers, precision=HI)
    turn = angles(own_pos - jnp.transpose(bead_centre), cluster_dirs)
    shifted = times_phase(samples, jnp.cos(turn), jnp.sin(turn))
    span_y = lax.axis_size("gy")
    code = (bead_ids // span_y - lax.axis_index("gx")) * 2 + (
        bead_ids % span_y - lax.axis_index("gy")
    )
    hot = (jnp.arange(4, dtype=jnp.int32)[:, None] == code[None, :]).astype(jnp.float32)
    part = jnp.einsum("kb,fbq->kfq", hot, shifted, precision=HI)
    part = part.reshape(2, 2, field_count, -1)
    section = part[:, 0] + shift(part[:, 1], "gy", 1)
    own = section[0] + shift(section[1], "gx", 1)
    half = own.shape[1] // 2
    halves = jnp.concatenate([own[:, :half], own[:, half:]], axis=0)
    by_real = jnp.dot(halves, cluster_waves[0], precision=HI)
    by_imag = jnp.dot(halves, cluster_waves[1], precision=HI)
    expansions = jnp.concatenate(
        [
            by_real[:field_count] - by_imag[field_count:],
            by_imag[:field_count] + by_real[field_count:],
        ],
        axis=1,
    )
    return (jnp.transpose(answer, (1, 0, 2))[None, None], expansions[None])


def solution(mesh):
    in_specs = (
        P("gx", "gy", None, None, None),
        P("gx", "gy", None, None),
        P("gx", "gy", None, None),
        P("gx", "gy", None, None),
        P("gx", "gy", None),
        P("gx", "gy", None),
        P(),
        P(),
        P(),
        P(),
        P(),
        P(),
    )
    out_specs = (P("gx", "gy", None, None, None), P(("gx", "gy"), None, None))
    return jax.shard_map(local, mesh=mesh, in_specs=in_specs, out_specs=out_specs, check_vma=False)
```

time: 811 us -> 152 us (0.19); the launches traced: 801 us -> 151 us
  blocking collectives: 368 us -> 39.9 us
  other arithmetic: 158 us -> 12.4 us
  waiting for transfers between devices: 118 us -> 30.9 us
  local copies, waits for them, and re-layouts: 89.7 us -> 14.2 us
    psum x5 -> x1, blocking collectives: 368 us -> 39.9 us  [local(): gram = lax.psum(gram, ('gx', 'gy'))]
    ppermute x14, waiting for transfers between devices: 118 us -> 30.9 us  [shift(): return lax.ppermute(block, axis, route)]
    gather x7 -> x0, local copies, waits for them, and re-layouts: 57.2 us -> none  [the longest x4 47 us: add_group(): wave_rows[flat_index[:, first_slot:first_slot + slot_width]]]
    convert_element_type x4, other arithmetic: 43.8 us -> 0.62 us  [the longest x2 0.41 us: scatter(): low = vector.astype(jnp.bfloat16)]
    sub x8 -> x2, other arithmetic: 43.4 us -> 1 us  [times_phase(): real_part * cos_part - imag_part * sin_part]
    reduce_sum x9 -> x2, other arithmetic: 34.7 us -> 1.94 us  [the longest x1 1.27 us: local(): jnp.sum((flat_index[:, :, None] == rows).astype(jnp.float32), axis=1)]
    mul x1, other arithmetic: 15.2 us -> 0.01 us  [weights(): return (y1 / beta + y2 * p, y2 * r)]
    concatenate x4 -> x0, other arithmetic: 10.8 us -> none  [extended(): block = jnp.concatenate([low, block, high], axis=dim)]
  transfers between devices with their start and end apart: 14 -> 14, of which waited for: 8 -> 10; matrix products, arithmetic and copies ran while one was open for 6% -> 10% of each run, Pallas kernels for 0% -> 0%
where the time goes in v1:
time: 152 us; the launch traced here: 151 us
  blocking collectives  39.9 us (26%)
  starting transfers between devices  37.1 us (24%)
  waiting for transfers between devices  30.9 us (20%)
  matrix products  14.4 us (9%)
  local copies, waits for them, and re-layouts  14.2 us (9%)
  other arithmetic  12.4 us (8%)
  between operations  1.59 us (1%)
    psum x1, blocking collectives, local(): gram = lax.psum(gram, ('gx', 'gy'))  39.9 us
    ppermute x14, starting transfers between devices, shift(): return lax.ppermute(block, axis, route)  37.1 us
    ppermute x14, waiting for transfers between devices, shift(): return lax.ppermute(block, axis, route)  30.9 us
    slice x1, local copies, waits for them, and re-layouts, local(): by_imag = jnp.dot(halves, cluster_waves[1], precision=HI)  6.69 us
    dot_general x1, matrix products, local(): jnp.einsum('fbc,cq->fbq', answer, block_matrix(to_cluster), precision=HI)  3.47 us
    unnamed x61, local copies, waits for them, and re-layouts  3.43 us
  transfers between devices with their start and end apart: 14, of which 10 were waited for; matrix products, arithmetic and copies ran while one was open for 10% of the time, Pallas kernels for 0%

profile of v1, /device:TPU:10, one launch (start us, length us, event | category | flops | bytes accessed | tf_op | source)
XLA Modules:
  0.0 150.6 jit_solution(8382609526279495677)
XLA Ops:
  3.2 3.3 %collective-permute-start.1 = (bf16[16,64,128]{2,1,0:T(8,128)(2,1)S(1)}, bf16[16,64,128]{2,1,0:T(8,128)(2,1)S(1)}, u32[]{:S(2)}, u32[]{:S(2)}) collective-permute-start(bf16[16,64,128]{2,1,0:T(8,128)(2,1)S(1)} %get-tuple-element.37), channel_id=1, source_target_pairs={{1,0},{2,1},{3,2},{4,3},{5,4},{6,5},{7,6},{9,8},{10,9},{11,10},{12... | collective-permute-start | bytes 786440 | tf_op jit(solution)/shard_map/ppermute | solution.py:20
  6.5 2.5 %collective-permute-start = (bf16[16,64,128]{2,1,0:T(8,128)(2,1)S(1)}, bf16[16,64,128]{2,1,0:T(8,128)(2,1)S(1)}, u32[]{:S(2)}, u32[]{:S(2)}) collective-permute-start(bf16[16,64,128]{2,1,0:T(8,128)(2,1)S(1)} %get-tuple-element.37), channel_id=1, source_target_pairs={{0,1},{1,2},{2,3},{3,4},{4,5},{5,6},{6,7},{8,9},{9,10},{10,11},{11... | collective-permute-start | bytes 786440 | tf_op jit(solution)/shard_map/ppermute | solution.py:20
  9.1 4.2 %collective-permute-start.5 = (f32[3,64]{1,0:T(4,128)S(1)}, f32[3,64]{1,0:T(4,128)S(1)}, u32[]{:S(2)}, u32[]{:S(2)}) collective-permute-start(f32[3,64]{1,0:T(4,128)S(1)} %bitcast.306), channel_id=1, source_target_pairs={{1,0},{2,1},{3,2},{4,3},{5,4},{6,5},{7,6},{9,8},{10,9},{11,10},{12... | collective-permute-start | bytes 2312 | tf_op jit(solution)/shard_map/ppermute | solution.py:20
  13.3 2.0 %collective-permute-start.4 = (f32[3,64]{1,0:T(4,128)S(1)}, f32[3,64]{1,0:T(4,128)S(1)}, u32[]{:S(2)}, u32[]{:S(2)}) collective-permute-start(f32[3,64]{1,0:T(4,128)S(1)} %bitcast.307), channel_id=1, source_target_pairs={{0,1},{1,2},{2,3},{3,4},{4,5},{5,6},{6,7},{8,9},{9,10},{10,11},{11... | collective-permute-start | bytes 2312 | tf_op jit(solution)/shard_map/ppermute | solution.py:20
  19.7 1.9 %collective-permute-start.7 = (f32[3,3,64]{2,1,0:T(4,128)S(1)}, f32[3,3,64]{2,1,0:T(4,128)S(1)}, u32[]{:S(2)}, u32[]{:S(2)}) collective-permute-start(f32[3,3,64]{2,1,0:T(4,128)S(1)} %get-tuple-element.76), channel_id=1, source_target_pairs={{8,0},{16,8},{24,16},{9,1},{17,9},{25,17},{10,2},{18,10},{26,18},{... | collective-permute-start | bytes 6920 | tf_op jit(solution)/shard_map/ppermute | solution.py:20
  21.6 2.4 %collective-permute-start.6 = (f32[3,3,64]{2,1,0:T(4,128)S(1)}, f32[3,3,64]{2,1,0:T(4,128)S(1)}, u32[]{:S(2)}, u32[]{:S(2)}) collective-permute-start(f32[3,3,64]{2,1,0:T(4,128)S(1)} %get-tuple-element.76), channel_id=1, source_target_pairs={{0,8},{8,16},{16,24},{1,9},{9,17},{17,25},{2,10},{10,18},{18,26},{... | collective-permute-start | bytes 6920 | tf_op jit(solution)/shard_map/ppermute | solution.py:20
  24.3 2.2 %collective-permute-done.6 = f32[3,3,64]{2,1,0:T(4,128)S(1)} collective-permute-done((f32[3,3,64]{2,1,0:T(4,128)S(1)}, f32[3,3,64]{2,1,0:T(4,128)S(1)}, u32[]{:S(2)}, u32[]{:S(2)}) %collective-permute-start.6) | collective-permute-done | bytes 2336 | tf_op jit(solution)/shard_map/ppermute | solution.py:20
  27.4 1.9 %collective-permute-start.3 = (bf16[3,16,64,128]{3,2,1,0:T(8,128)(2,1)S(1)}, bf16[3,16,64,128]{3,2,1,0:T(8,128)(2,1)S(1)}, u32[]{:S(2)}, u32[]{:S(2)}) collective-permute-start(bf16[3,16,64,128]{3,2,1,0:T(8,128)(2,1)S(1)} %pad_maximum_fusion), channel_id=1, source_target_pairs={{8,0},{16,8},{24,16},{9,1},{17,9},{25,17},{10,2},{18,10},{26,18},{... | collective-permute-start | bytes 2359304 | tf_op jit(solution)/shard_map/ppermute | solution.py:20
  29.4 2.5 %collective-permute-start.2 = (bf16[3,16,64,128]{3,2,1,0:T(8,128)(2,1)S(1)}, bf16[3,16,64,128]{3,2,1,0:T(8,128)(2,1)S(1)}, u32[]{:S(2)}, u32[]{:S(2)}) collective-permute-start(bf16[3,16,64,128]{3,2,1,0:T(8,128)(2,1)S(1)} %pad_maximum_fusion), channel_id=1, source_target_pairs={{0,8},{8,16},{16,24},{1,9},{9,17},{17,25},{2,10},{10,18},{18,26},{... | collective-permute-start | bytes 2359304 | tf_op jit(solution)/shard_map/ppermute | solution.py:20
  33.4 5.4 %collective-permute-done.3 = bf16[3,16,64,128]{3,2,1,0:T(8,128)(2,1)S(1)} collective-permute-done((bf16[3,16,64,128]{3,2,1,0:T(8,128)(2,1)S(1)}, bf16[3,16,64,128]{3,2,1,0:T(8,128)(2,1)S(1)}, u32[]{:S(2)}, u32[]{:S(2)}) %collective-permute-start.3) | collective-permute-done | bytes 786464 | tf_op jit(solution)/shard_map/ppermute | solution.py:20
  38.9 3.8 %collective-permute-done.2 = bf16[3,16,64,128]{3,2,1,0:T(8,128)(2,1)S(1)} collective-permute-done((bf16[3,16,64,128]{3,2,1,0:T(8,128)(2,1)S(1)}, bf16[3,16,64,128]{3,2,1,0:T(8,128)(2,1)S(1)}, u32[]{:S(2)}, u32[]{:S(2)}) %collective-permute-start.2) | collective-permute-done | bytes 786464 | tf_op jit(solution)/shard_map/ppermute | solution.py:20
  43.5 1.4 fusion.48
  44.8 1.3 subtract_convert_fusion.1
  48.5 3.5 %collective-permute-start.9 = (bf16[16,64,128]{2,1,0:T(8,128)(2,1)S(1)}, bf16[16,64,128]{2,1,0:T(8,128)(2,1)S(1)}, u32[]{:S(2)}, u32[]{:S(2)}) collective-permute-start(bf16[16,64,128]{2,1,0:T(8,128)(2,1)S(1)} %get-tuple-element.29), channel_id=1, source_target_pairs={{1,0},{2,1},{3,2},{4,3},{5,4},{6,5},{7,6},{9,8},{10,9},{11,10},{12... | collective-permute-start | bytes 786440 | tf_op jit(solution)/shard_map/ppermute | solution.py:20
  52.0 2.3 %collective-permute-start.8 = (bf16[16,64,128]{2,1,0:T(8,128)(2,1)S(1)}, bf16[16,64,128]{2,1,0:T(8,128)(2,1)S(1)}, u32[]{:S(2)}, u32[]{:S(2)}) collective-permute-start(bf16[16,64,128]{2,1,0:T(8,128)(2,1)S(1)} %get-tuple-element.29), channel_id=1, source_target_pairs={{0,1},{1,2},{2,3},{3,4},{4,5},{5,6},{6,7},{8,9},{9,10},{10,11},{11... | collective-permute-start | bytes 786440 | tf_op jit(solution)/shard_map/ppermute | solution.py:20
  54.8 2.0 %collective-permute-done.9 = bf16[16,64,128]{2,1,0:T(8,128)(2,1)S(1)} collective-permute-done((bf16[16,64,128]{2,1,0:T(8,128)(2,1)S(1)}, bf16[16,64,128]{2,1,0:T(8,128)(2,1)S(1)}, u32[]{:S(2)}, u32[]{:S(2)}) %collective-permute-start.9) | collective-permute-done | bytes 262176 | tf_op jit(solution)/shard_map/ppermute | solution.py:20
  56.8 4.4 %collective-permute-done.8 = bf16[16,64,128]{2,1,0:T(8,128)(2,1)S(1)} collective-permute-done((bf16[16,64,128]{2,1,0:T(8,128)(2,1)S(1)}, bf16[16,64,128]{2,1,0:T(8,128)(2,1)S(1)}, u32[]{:S(2)}, u32[]{:S(2)}) %collective-permute-start.8) | collective-permute-done | bytes 262176 | tf_op jit(solution)/shard_map/ppermute | solution.py:20
  61.4 1.9 %collective-permute-start.11 = (bf16[3,16,64,128]{3,2,1,0:T(8,128)(2,1)S(1)}, bf16[3,16,64,128]{3,2,1,0:T(8,128)(2,1)S(1)}, u32[]{:S(2)}, u32[]{:S(2)}) collective-permute-start(bf16[3,16,64,128]{3,2,1,0:T(8,128)(2,1)S(1)} %pad_maximum_fusion.1), channel_id=1, source_target_pairs={{8,0},{16,8},{24,16},{9,1},{17,9},{25,17},{10,2},{18,10},{26,18},{... | collective-permute-start | bytes 2359304 | tf_op jit(solution)/shard_map/ppermute | solution.py:20
  63.3 2.6 %collective-permute-start.10 = (bf16[3,16,64,128]{3,2,1,0:T(8,128)(2,1)S(1)}, bf16[3,16,64,128]{3,2,1,0:T(8,128)(2,1)S(1)}, u32[]{:S(2)}, u32[]{:S(2)}) collective-permute-start(bf16[3,16,64,128]{3,2,1,0:T(8,128)(2,1)S(1)} %pad_maximum_fusion.1), channel_id=1, source_target_pairs={{0,8},{8,16},{16,24},{1,9},{9,17},{17,25},{2,10},{10,18},{18,26},{... | collective-permute-start | bytes 2359304 | tf_op jit(solution)/shard_map/ppermute | solution.py:20
  67.4 5.4 %collective-permute-done.11 = bf16[3,16,64,128]{3,2,1,0:T(8,128)(2,1)S(1)} collective-permute-done((bf16[3,16,64,128]{3,2,1,0:T(8,128)(2,1)S(1)}, bf16[3,16,64,128]{3,2,1,0:T(8,128)(2,1)S(1)}, u32[]{:S(2)}, u32[]{:S(2)}) %collective-permute-start.11) | collective-permute-done | bytes 786464 | tf_op jit(solution)/shard_map/ppermute | solution.py:20
  72.8 3.8 %collective-permute-done.10 = bf16[3,16,64,128]{3,2,1,0:T(8,128)(2,1)S(1)} collective-permute-done((bf16[3,16,64,128]{3,2,1,0:T(8,128)(2,1)S(1)}, bf16[3,16,64,128]{3,2,1,0:T(8,128)(2,1)S(1)}, u32[]{:S(2)}, u32[]{:S(2)}) %collective-permute-start.10) | collective-permute-done | bytes 786464 | tf_op jit(solution)/shard_map/ppermute | solution.py:20
  77.7 1.4 fusion.47
  79.0 1.3 subtract_convert_fusion
  83.6 39.9 %psum.7 = f32[6,16]{1,0:T(8,128)S(1)} all-reduce(f32[6,16]{1,0:T(8,128)S(1)} %stack.113), channel_id=1, replica_groups=mesh['gx'=4,'gy'=8] {'gx','gy'}, use_global_device_ids=true, to_apply=%region_7.8 | all-reduce | flops 96 | bytes 768 | tf_op jit(solution)/shard_map/psum | solution.py:161
  123.6 3.5 %fusion.29 = f32[16,64,1024]{2,1,0:T(8,128)S(1)} fusion(f32[64,512]{1,0:T(8,128)S(1)} %copy-done.3, f32[64,512]{1,0:T(8,128)S(1)} %fusion.94, f32[64,512]{1,0:T(8,128)S(1)} %get-tuple-element.61, f32[16,64,128]{2,1,0:T(8,128)S(1)} %get-tuple-element.30, f32[16,64,128]{2,1,0:T(8,128)S(1)} %get-tuple-element.38, f32[16]{0:T(128)S(1)} %mul.1284, ...), kind=kOutput, calls=%fused_computation.46 | convolution fusion | flops 1611399168 | bytes 5636224 | tf_op jit(solution)/shard_map/fbc,cq->fbq/dot_general | solution.py:166
  127.9 1.5 fusion.8
  129.9 3.8 %collective-permute-start.12 = (f32[2,16,1024]{2,0,1:T(2,128)S(1)}, f32[2,16,1024]{2,0,1:T(2,128)S(1)}, u32[]{:S(2)}, u32[]{:S(2)}) collective-permute-start(f32[2,16,1024]{2,0,1:T(2,128)S(1)} %bitcast.299), channel_id=1, source_target_pairs={{0,1},{1,2},{2,3},{3,4},{4,5},{5,6},{6,7},{8,9},{9,10},{10,11},{11... | collective-permute-start | bytes 393224 | tf_op jit(solution)/shard_map/ppermute | solution.py:20
  133.7 6.7 %fusion.103 = (f32[1,512,961]{1,0,2:T(1,128)S(1)}, f32[1,512,961]{1,0,2:T(1,128)S(1)}) fusion(f32[2,512,961]{1,0,2:T(2,128)} %param.22), kind=kLoop, calls=%fused_computation.223 | loop fusion | bytes 7872512 | tf_op jit(solution)/shard_map/slice | solution.py:187
  140.6 2.1 %collective-permute-start.13 = (f32[16,1024]{1,0:T(8,128)S(1)}, f32[16,1024]{1,0:T(8,128)S(1)}, u32[]{:S(2)}, u32[]{:S(2)}) collective-permute-start(f32[16,1024]{1,0:T(8,128)S(1)} %bitcast.302), channel_id=1, source_target_pairs={{0,8},{8,16},{16,24},{1,9},{9,17},{17,25},{2,10},{10,18},{18,26},{... | collective-permute-start | bytes 196616 | tf_op jit(solution)/shard_map/ppermute | solution.py:20
  144.0 2.2 %collective-permute-done.13 = f32[16,1024]{1,0:T(8,128)S(1)} collective-permute-done((f32[16,1024]{1,0:T(8,128)S(1)}, f32[16,1024]{1,0:T(8,128)S(1)}, u32[]{:S(2)}, u32[]{:S(2)}) %collective-permute-start.13) | collective-permute-done | bytes 65568 | tf_op jit(solution)/shard_map/ppermute | solution.py:20
  146.3 1.8 %fusion.12 = f32[32,961]{1,0:T(8,128)S(1)} fusion(f32[1,512,961]{1,0,2:T(1,128)S(1)} %get-tuple-element.45, f32[16,512]{1,0:T(8,128)S(1)} %get-tuple-element.66, f32[16,512]{1,0:T(8,128)S(1)} %get-tuple-element.65), kind=kOutput, calls=%fused_computation.23 | convolution fusion | flops 188956672 | bytes 2156672 | tf_op jit(solution)/shard_map/dot_general | solution.py:187
  148.0 1.8 %fusion.13 = f32[32,961]{1,0:T(8,128)S(1)} fusion(f32[1,512,961]{1,0,2:T(1,128)S(1)} %get-tuple-element.46, f32[16,512]{1,0:T(8,128)S(1)} %get-tuple-element.66, f32[16,512]{1,0:T(8,128)S(1)} %get-tuple-element.65), kind=kOutput, calls=%fused_computation.25 | convolution fusion | flops 188956672 | bytes 2156672 | tf_op jit(solution)/shard_map/dot_general | solution.py:186
  (147 shorter events, 22.1 us)
Async XLA Ops:
  0.6 17.2 %copy-start = (f32[32,3]{0,1:T(4,128)S(1)}, f32[32,3]{0,1:T(4,128)}, u32[]{:S(2)}) copy-start(f32[32,3]{0,1:T(4,128)} %param.23) | copy-start | bytes 1156
  2.6 6.4 %copy-start.24 = (f32[1,1,3,64]{3,1,2,0:T(1,128)S(1)}, f32[1,1,3,64]{3,1,2,0:T(1,128)}, u32[]{:S(2)}) copy-start(f32[1,1,3,64]{3,1,2,0:T(1,128)} %param.13) | copy-start | bytes 2308
  2.6 12.7 %copy-start.16 = (bf16[2,64,128]{2,1,0:T(8,128)(2,1)S(1)}, bf16[2,64,128]{2,1,0:T(8,128)(2,1)}, u32[]{:S(2)}) copy-start(bf16[2,64,128]{2,1,0:T(8,128)(2,1)} %param.19) | copy-start | bytes 98308
  2.6 13.3 %copy-start.22 = (s32[1,1,64,60]{2,1,3,0:T(1,128)S(1)}, s32[1,1,64,60]{2,1,3,0:T(1,128)}, u32[]{:S(2)}) copy-start(s32[1,1,64,60]{2,1,3,0:T(1,128)} %param.15) | copy-start | bytes 46084
  2.7 13.3 %copy-start.23 = (s32[1,1,64,60]{2,1,3,0:T(1,128)S(1)}, s32[1,1,64,60]{2,1,3,0:T(1,128)}, u32[]{:S(2)}) copy-start(s32[1,1,64,60]{2,1,3,0:T(1,128)} %param.14) | copy-start | bytes 46084
  2.7 13.4 %copy-start.25 = (s32[1,1,64]{2,1,0:T(1,128)S(1)}, s32[1,1,64]{2,1,0:T(1,128)}, u32[]{:S(2)}) copy-start(s32[1,1,64]{2,1,0:T(1,128)} %param.16) | copy-start | bytes 772
  2.7 14.7 %copy-start.19 = (bf16[2,128,64]{1,2,0:T(8,128)(2,1)S(1)}, bf16[2,128,64]{1,2,0:T(8,128)(2,1)}, u32[]{:S(2)}) copy-start(bf16[2,128,64]{1,2,0:T(8,128)(2,1)} %param.20) | copy-start | bytes 98308
  2.7 15.2 %copy-start.26 = (s32[1,1,64]{2,1,0:T(1,128)S(1)}, s32[1,1,64]{2,1,0:T(1,128)}, u32[]{:S(2)}) copy-start(s32[1,1,64]{2,1,0:T(1,128)} %param.17) | copy-start | bytes 772
  3.2 24.0 %collective-permute-start.1 = (bf16[16,64,128]{2,1,0:T(8,128)(2,1)S(1)}, bf16[16,64,128]{2,1,0:T(8,128)(2,1)S(1)}, u32[]{:S(2)}, u32[]{:S(2)}) collective-permute-start(bf16[16,64,128]{2,1,0:T(8,128)(2,1)S(1)} %get-tuple-element.37), channel_id=1, source_target_pairs={{1,0},{2,1},{3,2},{4,3},{5,4},{6,5},{7,6},{9,8},{10,9},{11,10},{12... | collective-permute-start | bytes 786440 | tf_op jit(solution)/shard_map/ppermute | solution.py:20
  6.5 20.7 %collective-permute-start = (bf16[16,64,128]{2,1,0:T(8,128)(2,1)S(1)}, bf16[16,64,128]{2,1,0:T(8,128)(2,1)S(1)}, u32[]{:S(2)}, u32[]{:S(2)}) collective-permute-start(bf16[16,64,128]{2,1,0:T(8,128)(2,1)S(1)} %get-tuple-element.37), channel_id=1, source_target_pairs={{0,1},{1,2},{2,3},{3,4},{4,5},{5,6},{6,7},{8,9},{9,10},{10,11},{11... | collective-permute-start | bytes 786440 | tf_op jit(solution)/shard_map/ppermute | solution.py:20
  9.1 9.7 %collective-permute-start.5 = (f32[3,64]{1,0:T(4,128)S(1)}, f32[3,64]{1,0:T(4,128)S(1)}, u32[]{:S(2)}, u32[]{:S(2)}) collective-permute-start(f32[3,64]{1,0:T(4,128)S(1)} %bitcast.306), channel_id=1, source_target_pairs={{1,0},{2,1},{3,2},{4,3},{5,4},{6,5},{7,6},{9,8},{10,9},{11,10},{12... | collective-permute-start | bytes 2312 | tf_op jit(solution)/shard_map/ppermute | solution.py:20
  13.3 6.4 %collective-permute-start.4 = (f32[3,64]{1,0:T(4,128)S(1)}, f32[3,64]{1,0:T(4,128)S(1)}, u32[]{:S(2)}, u32[]{:S(2)}) collective-permute-start(f32[3,64]{1,0:T(4,128)S(1)} %bitcast.307), channel_id=1, source_target_pairs={{0,1},{1,2},{2,3},{3,4},{4,5},{5,6},{6,7},{8,9},{9,10},{10,11},{11... | collective-permute-start | bytes 2312 | tf_op jit(solution)/shard_map/ppermute | solution.py:20
  15.4 28.1 %copy-start.6 = (bf16[64,128]{1,0:T(8,128)(2,1)}, bf16[64,128]{1,0:T(8,128)(2,1)S(1)}, u32[]{:S(2)}) copy-start(bf16[64,128]{1,0:T(8,128)(2,1)S(1)} %get-tuple-element.69) | copy-start | bytes 49156
  15.4 28.1 %copy-start.8 = (bf16[64,128]{1,0:T(8,128)(2,1)}, bf16[64,128]{1,0:T(8,128)(2,1)S(1)}, u32[]{:S(2)}) copy-start(bf16[64,128]{1,0:T(8,128)(2,1)S(1)} %get-tuple-element.70) | copy-start | bytes 49156
  15.4 28.1 %copy-start.4 = (bf16[64,128]{1,0:T(8,128)(2,1)}, bf16[64,128]{1,0:T(8,128)(2,1)S(1)}, u32[]{:S(2)}) copy-start(bf16[64,128]{1,0:T(8,128)(2,1)S(1)} %fusion.92) | copy-start | bytes 49156
  17.5 30.1 %copy-start.14 = (bf16[1,128,64]{2,1,0:T(8,128)(2,1)}, bf16[1,128,64]{2,1,0:T(8,128)(2,1)S(1)}, u32[]{:S(2)}) copy-start(bf16[1,128,64]{2,1,0:T(8,128)(2,1)S(1)} %copy.53) | copy-start | bytes 49156
  17.5 30.1 %copy-start.20 = (bf16[128,64]{1,0:T(8,128)(2,1)}, bf16[128,64]{1,0:T(8,128)(2,1)S(1)}, u32[]{:S(2)}) copy-start(bf16[128,64]{1,0:T(8,128)(2,1)S(1)} %bitcast_negate_fusion) | copy-start | bytes 49156
  19.7 4.6 %collective-permute-start.7 = (f32[3,3,64]{2,1,0:T(4,128)S(1)}, f32[3,3,64]{2,1,0:T(4,128)S(1)}, u32[]{:S(2)}, u32[]{:S(2)}) collective-permute-start(f32[3,3,64]{2,1,0:T(4,128)S(1)} %get-tuple-element.76), channel_id=1, source_target_pairs={{8,0},{16,8},{24,16},{9,1},{17,9},{25,17},{10,2},{18,10},{26,18},{... | collective-permute-start | bytes 6920 | tf_op jit(solution)/shard_map/ppermute | solution.py:20
  21.6 4.9 %collective-permute-start.6 = (f32[3,3,64]{2,1,0:T(4,128)S(1)}, f32[3,3,64]{2,1,0:T(4,128)S(1)}, u32[]{:S(2)}, u32[]{:S(2)}) collective-permute-start(f32[3,3,64]{2,1,0:T(4,128)S(1)} %get-tuple-element.76), channel_id=1, source_target_pairs={{0,8},{8,16},{16,24},{1,9},{9,17},{17,25},{2,10},{10,18},{18,26},{... | collective-permute-start | bytes 6920 | tf_op jit(solution)/shard_map/ppermute | solution.py:20
  24.3 23.4 %copy-start.17 = (bf16[1,128,64]{2,1,0:T(8,128)(2,1)}, bf16[1,128,64]{2,1,0:T(8,128)(2,1)S(1)}, u32[]{:S(2)}) copy-start(bf16[1,128,64]{2,1,0:T(8,128)(2,1)S(1)} %copy.52) | copy-start | bytes 49156
  27.4 11.4 %collective-permute-start.3 = (bf16[3,16,64,128]{3,2,1,0:T(8,128)(2,1)S(1)}, bf16[3,16,64,128]{3,2,1,0:T(8,128)(2,1)S(1)}, u32[]{:S(2)}, u32[]{:S(2)}) collective-permute-start(bf16[3,16,64,128]{3,2,1,0:T(8,128)(2,1)S(1)} %pad_maximum_fusion), channel_id=1, source_target_pairs={{8,0},{16,8},{24,16},{9,1},{17,9},{25,17},{10,2},{18,10},{26,18},{... | collective-permute-start | bytes 2359304 | tf_op jit(solution)/shard_map/ppermute | solution.py:20
  29.4 13.3 %collective-permute-start.2 = (bf16[3,16,64,128]{3,2,1,0:T(8,128)(2,1)S(1)}, bf16[3,16,64,128]{3,2,1,0:T(8,128)(2,1)S(1)}, u32[]{:S(2)}, u32[]{:S(2)}) collective-permute-start(bf16[3,16,64,128]{3,2,1,0:T(8,128)(2,1)S(1)} %pad_maximum_fusion), channel_id=1, source_target_pairs={{0,8},{8,16},{16,24},{1,9},{9,17},{17,25},{2,10},{10,18},{18,26},{... | collective-permute-start | bytes 2359304 | tf_op jit(solution)/shard_map/ppermute | solution.py:20
  32.0 14.2 %copy-start.10 = (bf16[64,576]{0,1:T(8,128)(2,1)}, bf16[64,576]{0,1:T(8,128)(2,1)S(1)}, u32[]{:S(2)}) copy-start(bf16[64,576]{0,1:T(8,128)(2,1)S(1)} %get-tuple-element.31) | copy-start | bytes 221188
  32.1 14.1 %copy-start.12 = (bf16[64,576]{0,1:T(8,128)(2,1)}, bf16[64,576]{0,1:T(8,128)(2,1)S(1)}, u32[]{:S(2)}) copy-start(bf16[64,576]{0,1:T(8,128)(2,1)S(1)} %subtract_convert_fusion.4) | copy-start | bytes 221188
  48.0 6.7 %copy-start.2 = (f32[2,64,512]{2,1,0:T(8,128)S(1)}, f32[2,64,512]{2,1,0:T(8,128)}, u32[]{:S(2)}) copy-start(f32[2,64,512]{2,1,0:T(8,128)} %param.21) | copy-start | bytes 786436
  48.5 8.3 %collective-permute-start.9 = (bf16[16,64,128]{2,1,0:T(8,128)(2,1)S(1)}, bf16[16,64,128]{2,1,0:T(8,128)(2,1)S(1)}, u32[]{:S(2)}, u32[]{:S(2)}) collective-permute-start(bf16[16,64,128]{2,1,0:T(8,128)(2,1)S(1)} %get-tuple-element.29), channel_id=1, source_target_pairs={{1,0},{2,1},{3,2},{4,3},{5,4},{6,5},{7,6},{9,8},{10,9},{11,10},{12... | collective-permute-start | bytes 786440 | tf_op jit(solution)/shard_map/ppermute | solution.py:20
  52.0 9.2 %collective-permute-start.8 = (bf16[16,64,128]{2,1,0:T(8,128)(2,1)S(1)}, bf16[16,64,128]{2,1,0:T(8,128)(2,1)S(1)}, u32[]{:S(2)}, u32[]{:S(2)}) collective-permute-start(bf16[16,64,128]{2,1,0:T(8,128)(2,1)S(1)} %get-tuple-element.29), channel_id=1, source_target_pairs={{0,1},{1,2},{2,3},{3,4},{4,5},{5,6},{6,7},{8,9},{9,10},{10,11},{11... | collective-permute-start | bytes 786440 | tf_op jit(solution)/shard_map/ppermute | solution.py:20
  61.4 11.4 %collective-permute-start.11 = (bf16[3,16,64,128]{3,2,1,0:T(8,128)(2,1)S(1)}, bf16[3,16,64,128]{3,2,1,0:T(8,128)(2,1)S(1)}, u32[]{:S(2)}, u32[]{:S(2)}) collective-permute-start(bf16[3,16,64,128]{3,2,1,0:T(8,128)(2,1)S(1)} %pad_maximum_fusion.1), channel_id=1, source_target_pairs={{8,0},{16,8},{24,16},{9,1},{17,9},{25,17},{10,2},{18,10},{26,18},{... | collective-permute-start | bytes 2359304 | tf_op jit(solution)/shard_map/ppermute | solution.py:20
  63.3 13.3 %collective-permute-start.10 = (bf16[3,16,64,128]{3,2,1,0:T(8,128)(2,1)S(1)}, bf16[3,16,64,128]{3,2,1,0:T(8,128)(2,1)S(1)}, u32[]{:S(2)}, u32[]{:S(2)}) collective-permute-start(bf16[3,16,64,128]{3,2,1,0:T(8,128)(2,1)S(1)} %pad_maximum_fusion.1), channel_id=1, source_target_pairs={{0,8},{8,16},{16,24},{1,9},{9,17},{17,25},{2,10},{10,18},{18,26},{... | collective-permute-start | bytes 2359304 | tf_op jit(solution)/shard_map/ppermute | solution.py:20
  82.7 41.0 %copy-start.3 = (f32[64,512]{1,0:T(8,128)S(1)}, f32[64,512]{1,0:T(8,128)}, u32[]{:S(2)}) copy-start(f32[64,512]{1,0:T(8,128)} %get-tuple-element.62) | copy-start | bytes 393220
  129.9 10.5 %collective-permute-start.12 = (f32[2,16,1024]{2,0,1:T(2,128)S(1)}, f32[2,16,1024]{2,0,1:T(2,128)S(1)}, u32[]{:S(2)}, u32[]{:S(2)}) collective-permute-start(f32[2,16,1024]{2,0,1:T(2,128)S(1)} %bitcast.299), channel_id=1, source_target_pairs={{0,1},{1,2},{2,3},{3,4},{4,5},{5,6},{6,7},{8,9},{9,10},{10,11},{11... | collective-permute-start | bytes 393224 | tf_op jit(solution)/shard_map/ppermute | solution.py:20
  140.6 5.6 %collective-permute-start.13 = (f32[16,1024]{1,0:T(8,128)S(1)}, f32[16,1024]{1,0:T(8,128)S(1)}, u32[]{:S(2)}, u32[]{:S(2)}) collective-permute-start(f32[16,1024]{1,0:T(8,128)S(1)} %bitcast.302), channel_id=1, source_target_pairs={{0,8},{8,16},{16,24},{1,9},{9,17},{17,25},{2,10},{10,18},{18,26},{... | collective-permute-start | bytes 196616 | tf_op jit(solution)/shard_map/ppermute | solution.py:20
  (9 other events, 11.5 us)

commit v2 on v1

--- a/solution.py
+++ b/solution.py
@@ -1,8 +1,11 @@
+import functools
 import math
 
 import jax
 import jax.numpy as jnp
 from jax import lax
+from jax.experimental import pallas as pl
+from jax.experimental.pallas import tpu as pltpu
 from jax.sharding import PartitionSpec as P
 
 WAVE_LAT = 8
@@ -18,11 +21,6 @@
     count = lax.axis_size(axis)
     route = [(i - distance, i) for i in range(count) if 0 <= i - distance < count]
     return lax.ppermute(block, axis, route)
-
-
-def extended(block):
-    column = jnp.stack([shift(block, "gy", 1), block, shift(block, "gy", -1)])
-    return jnp.stack([shift(column, "gx", 1), column, shift(column, "gx", -1)])
 
 
 def sphere_grid(cycle_count, cycle_size):
@@ -89,6 +87,292 @@
     return y1 / beta + y2 * p, y2 * r
 
 
+CHUNKS = 2
+SHIFTS = [(dx, dy) for dx in (-1, 0, 1) for dy in (-1, 0, 1)]
+
+
+def krylov_kernel(
+    nx,
+    ny,
+    source,
+    column_pos,
+    row_pos,
+    times,
+    dirs,
+    forward_matrix,
+    back_matrix,
+    mie_rows,
+    once,
+    gram_out,
+    buf_one,
+    buf_two,
+    geo,
+    turn_cos,
+    turn_sin,
+    weight,
+    total,
+    gram_x,
+    gram_y,
+    geo_send,
+    geo_recv,
+    one_send,
+    one_recv,
+    two_send,
+    two_recv,
+    x_send,
+    x_recv,
+    y_send,
+    y_recv,
+):
+    i, j = lax.axis_index("gx"), lax.axis_index("gy")
+    fields, beads, width = source.shape
+    wide = turn_cos.shape[2]
+    step = fields // CHUNKS
+
+    def present(dx, dy):
+        return (i + dx >= 0) & (i + dx < nx) & (j + dy >= 0) & (j + dy < ny)
+
+    def piece(buf, p, c):
+        if len(buf.shape) == 3:
+            return buf.at[p]
+        return buf.at[pl.ds(c * step, step), p]
+
+    def make(buf, send, recv, slot, src, dst, c, dx, dy):
+        return pltpu.make_async_remote_copy(
+            src_ref=piece(buf, src, c),
+            dst_ref=piece(buf, dst, c),
+            send_sem=send.at[slot, c],
+            recv_sem=recv.at[dst, c],
+            device_id=(i + dx, j + dy),
+            device_id_type=pl.DeviceIdType.MESH,
+        )
+
+    own_routes = [(0, 4, 3, 0, 1), (1, 4, 5, 0, -1), (2, 4, 1, 1, 0), (3, 4, 7, -1, 0)]
+    low_routes = [(4, 3, 0, 1, 0), (5, 3, 6, -1, 0)]
+    high_routes = [(6, 5, 2, 1, 0), (7, 5, 8, -1, 0)]
+
+    def guarded(route):
+        ok = present(route[3], route[4])
+        if route[1] == 3:
+            ok = ok & (j > 0)
+        if route[1] == 5:
+            ok = ok & (j < ny - 1)
+        return pl.when(ok)
+
+    def start(group, routes, c):
+        for route in routes:
+
+            @guarded(route)
+            def _(route=route):
+                slot, src, dst, dx, dy = route
+                make(*group, slot, src, dst, c, dx, dy).start()
+
+    def finish_sends(group, count):
+        for c in range(count):
+            for route in own_routes + low_routes + high_routes:
+
+                @guarded(route)
+                def _(route=route, c=c):
+                    slot, src, dst, dx, dy = route
+                    make(*group, slot, src, dst, c, dx, dy).wait_send()
+
+    def arrive(group, p, c):
+        dx, dy = SHIFTS[p]
+        via = (dx, 0) if dx != 0 else (0, dy)
+
+        @pl.when(present(dx, dy))
+        def _():
+            make(*group, 0, 4, p, c, via[0], via[1]).wait_recv()
+
+    def forward(group, c):
+        arrive(group, 3, c)
+        start(group, low_routes, c)
+        arrive(group, 5, c)
+        start(group, high_routes, c)
+
+    geo_group = (geo, geo_send, geo_recv)
+    one_group = (buf_one, one_send, one_recv)
+    two_group = (buf_two, two_send, two_recv)
+
+    barrier = pltpu.get_barrier_semaphore()
+    for d in range(1, nx):
+        pl.semaphore_signal(
+            barrier,
+            inc=1,
+            device_id=(lax.rem(i + d, nx), j),
+            device_id_type=pl.DeviceIdType.MESH,
+        )
+    for d in range(1, ny):
+        pl.semaphore_signal(
+            barrier,
+            inc=1,
+            device_id=(i, lax.rem(j + d, ny)),
+            device_id_type=pl.DeviceIdType.MESH,
+        )
+    geo[4] = column_pos[...]
+
+    def to_low(f, carry):
+        buf_one[f, 4] = source[f].astype(jnp.bfloat16)
+        return carry
+
+    lax.fori_loop(0, fields, to_low, 0)
+    for p, (dx, dy) in enumerate(SHIFTS):
+
+        @pl.when(jnp.logical_not(present(dx, dy)))
+        def _(p=p):
+            geo[p] = jnp.zeros(geo.shape[1:], geo.dtype)
+
+            def clear(f, carry):
+                buf_one[f, p] = jnp.zeros((beads, width), jnp.bfloat16)
+                buf_two[f, p] = jnp.zeros((beads, width), jnp.bfloat16)
+                return carry
+
+            lax.fori_loop(0, fields, clear, 0)
+
+    pl.semaphore_wait(barrier, nx + ny - 2)
+
+    start(geo_group, own_routes, 0)
+    for c in range(CHUNKS):
+        start(one_group, own_routes, c)
+    forward(geo_group, 0)
+
+    def geometry(p):
+        pos = geo[p]
+        along = (
+            pos[:, 0:1] * dirs[0:1, :] + pos[:, 1:2] * dirs[1:2, :] + pos[:, 2:3] * dirs[2:3, :]
+        )
+        angle = WAVENUMBER * along
+        turn_cos[p] = jnp.cos(angle)
+        turn_sin[p] = jnp.sin(angle)
+        ex = row_pos[0:1, :] - pos[:, 0:1]
+        ey = row_pos[1:2, :] - pos[:, 1:2]
+        ez = row_pos[2:3, :] - pos[:, 2:3]
+        dist = jnp.sqrt(ex * ex + ey * ey + ez * ez)
+        full = times[p] / (1.0 + dist)
+        high = full.astype(jnp.bfloat16).astype(jnp.float32)
+        lane = lax.broadcasted_iota(jnp.int32, full.shape, 1)
+        weight[p] = jnp.where(lane < beads, high, full - high).astype(jnp.bfloat16)
+
+    geometry(4)
+    for p in (3, 5):
+        geometry(p)
+    for c in range(CHUNKS):
+        forward(one_group, c)
+    for p in (0, 1, 2, 6, 7, 8):
+        arrive(geo_group, p, 0)
+        geometry(p)
+
+    def gathered(buf, f, first, count):
+        rows = count * beads
+        spot = pl.ds(first, count)
+        low = buf[f, spot].reshape(rows, width)
+        smp = jnp.dot(low, forward_matrix[...], preferred_element_type=jnp.float32)
+        re, im = smp[:, :wide], smp[:, wide:]
+        co = turn_cos[spot].reshape(rows, wide)
+        si = turn_sin[spot].reshape(rows, wide)
+        turned = jnp.concatenate(
+            [
+                (re * co + im * si).astype(jnp.bfloat16),
+                (im * co - re * si).astype(jnp.bfloat16),
+            ],
+            axis=1,
+        )
+        return lax.dot_general(
+            weight[spot].reshape(rows, 2 * beads),
+            turned,
+            (((0,), (0,)), ((), ())),
+            preferred_element_type=jnp.float32,
+        )
+
+    def back_turn(acc):
+        inc = acc[:beads] + acc[beads:]
+        re, im = inc[:, :wide], inc[:, wide:]
+        co, si = turn_cos[4], turn_sin[4]
+        inc = jnp.concatenate([re * co - im * si, re * si + im * co], axis=1)
+        high = inc.astype(jnp.bfloat16)
+        low = (inc - high.astype(jnp.float32)).astype(jnp.bfloat16)
+        back = jnp.dot(
+            jnp.concatenate([high, low], axis=0),
+            back_matrix[...],
+            preferred_element_type=jnp.float32,
+        )
+        back = back[:beads] + back[beads:]
+        return back * mie_rows[0:1, :] + pltpu.roll(back, width // 2, 1) * mie_rows[1:2, :]
+
+    def middle(buf):
+        def body(f, carry):
+            total[f] = gathered(buf, f, 3, 3)
+            return carry
+
+        lax.fori_loop(0, fields, body, 0)
+
+    def sides(buf, f):
+        return back_turn(total[f] + gathered(buf, f, 0, 3) + gathered(buf, f, 6, 3))
+
+    middle(buf_one)
+    for c in range(CHUNKS):
+        for p in (0, 1, 2, 6, 7, 8):
+            arrive(one_group, p, c)
+
+        def first(f, carry):
+            value = sides(buf_one, f)
+            once[f] = value
+            buf_two[f, 4] = value.astype(jnp.bfloat16)
+            return carry
+
+        lax.fori_loop(c * step, (c + 1) * step, first, 0)
+        start(two_group, own_routes, c)
+
+    for c in range(CHUNKS):
+        forward(two_group, c)
+    middle(buf_two)
+
+    row = lax.broadcasted_iota(jnp.int32, (8, 128), 0)
+    lane = lax.broadcasted_iota(jnp.int32, (8, 128), 1)
+    gram = jnp.zeros((8, 128), jnp.float32)
+    for c in range(CHUNKS):
+        for p in (0, 1, 2, 6, 7, 8):
+            arrive(two_group, p, c)
+
+        def second(f, gram):
+            u = sides(buf_two, f)
+            s, t = source[f], once[f]
+            for k, (x, y) in enumerate(((s, s), (s, t), (t, t), (s, u), (t, u), (u, u))):
+                value = jnp.sum(jnp.sum(x * y, axis=0, keepdims=True), axis=1, keepdims=True)
+                gram = gram + jnp.where((row == k) & (lane == f), value, 0.0)
+            return gram
+
+        gram = lax.fori_loop(c * step, (c + 1) * step, second, gram)
+
+    def reduce_over(gram, slots, send, recv, count, peer):
+        slots[0] = gram
+        copies = []
+        for d in range(1, count):
+            copy = pltpu.make_async_remote_copy(
+                src_ref=slots.at[0],
+                dst_ref=slots.at[d],
+                send_sem=send.at[d],
+                recv_sem=recv.at[d],
+                device_id=peer(d),
+                device_id_type=pl.DeviceIdType.MESH,
+            )
+            copy.start()
+            copies.append(copy)
+        for d, copy in enumerate(copies):
+            copy.wait_recv()
+            gram = gram + slots[d + 1]
+        for copy in copies:
+            copy.wait_send()
+        return gram
+
+    gram = reduce_over(gram, gram_x, x_send, x_recv, nx, lambda d: (lax.rem(i + d, nx), j))
+    gram = reduce_over(gram, gram_y, y_send, y_recv, ny, lambda d: (i, lax.rem(j + d, ny)))
+    gram_out[...] = gram
+    finish_sends(geo_group, 1)
+    finish_sends(one_group, CHUNKS)
+    finish_sends(two_group, CHUNKS)
+
+
 def local(
     incident,
     positions,
@@ -111,55 +395,60 @@
     back_matrix = block_matrix(from_waves)
     source = times_phase(jnp.transpose(incident[0, 0], (1, 0, 2)), mie[0], mie[1])
     own_pos = positions[0, 0]
-    all_pos = jnp.transpose(extended(own_pos), (2, 0, 1, 3)).reshape(3, 9 * bead_count)
     flat_index = nbr_part[0, 0] * bead_count + nbr_slot[0, 0]
     slots = jnp.arange(flat_index.shape[1], dtype=jnp.int32)
     flat_index = jnp.where(slots[None, :] < nbr_count[0, 0][:, None], flat_index, -1)
+    flat_index = jnp.transpose(flat_index)
+    flat_index = jnp.concatenate([flat_index, flat_index], axis=1)
     rows = jnp.arange(9 * bead_count, dtype=jnp.int32)
-    times = jnp.sum((flat_index[:, :, None] == rows).astype(jnp.float32), axis=1)
-    diff = own_pos[:, :, None] - all_pos[:, None, :]
-    dist = jnp.sqrt(diff[0] * diff[0] + diff[1] * diff[1] + diff[2] * diff[2])
-    weight = times / (1.0 + dist)
-    weight_hi = weight.astype(jnp.bfloat16)
-    weight_lo = (weight - weight_hi.astype(jnp.float32)).astype(jnp.bfloat16)
-    weight_pair = jnp.concatenate([weight_hi, weight_lo], axis=0)
-    dirs = sphere_grid(WAVE_LAT, WAVE_LON)
-    own_angle = angles(own_pos, dirs)
-    own_cos, own_sin = jnp.cos(own_angle), jnp.sin(own_angle)
-    all_angle = angles(all_pos, dirs)
-    all_cos, all_sin = jnp.cos(all_angle), jnp.sin(all_angle)
-
-    def scatter(vector):
-        low = vector.astype(jnp.bfloat16)
-        blocks = extended(low)
-        blocks = jnp.transpose(blocks, (2, 0, 1, 3, 4)).reshape(
-            field_count, 9 * bead_count, coef_width
-        )
-        samples = jnp.einsum(
-            "fnc,cq->fnq", blocks, forward_matrix, preferred_element_type=jnp.float32
-        )
-        turned = times_phase(samples, all_cos, -all_sin).astype(jnp.bfloat16)
-        both = jnp.einsum("bn,fnq->fbq", weight_pair, turned, preferred_element_type=jnp.float32)
-        incoming = both[:, :bead_count] + both[:, bead_count:]
-        incoming = times_phase(incoming, own_cos, own_sin).astype(jnp.bfloat16)
-        back = jnp.einsum(
-            "fbq,qc->fbc", incoming, back_matrix, preferred_element_type=jnp.float32
-        )
-        return times_phase(back, mie[0], mie[1])
-
-    once = scatter(source)
-    twice = scatter(once)
-    pairs = (
-        (source, source),
-        (source, once),
-        (once, once),
-        (source, twice),
-        (once, twice),
-        (twice, twice),
-    )
-    gram = jnp.stack([jnp.sum(x * y, axis=(1, 2)) for x, y in pairs])
-    gram = lax.psum(gram, ("gx", "gy"))
-    w_source, w_once = weights(gram)
+    times = jnp.sum((flat_index[:, None, :] == rows[None, :, None]).astype(jnp.float32), axis=0)
+    times = times.reshape(9, bead_count, 2 * bead_count)
+    dirs = jnp.pad(sphere_grid(WAVE_LAT, WAVE_LON), ((0, 5), (0, 0)))
+    column_pos = jnp.pad(jnp.transpose(own_pos), ((0, 0), (0, 125)))
+    row_pos = jnp.pad(jnp.concatenate([own_pos, own_pos], axis=1), ((0, 5), (0, 0)))
+    mie_rows = jnp.stack(
+        [jnp.concatenate([mie[0], mie[0]]), jnp.concatenate([-mie[1], mie[1]])]
+    )
+    mie_rows = jnp.pad(mie_rows, ((0, 6), (0, 0)))
+    nx, ny = lax.axis_size("gx"), lax.axis_size("gy")
+    vmem = pl.BlockSpec(memory_space=pltpu.VMEM)
+    dma = pltpu.SemaphoreType.DMA
+    blocks = (field_count, 9, bead_count, coef_width)
+    once, gram = pl.pallas_call(
+        functools.partial(krylov_kernel, nx, ny),
+        out_shape=(
+            jax.ShapeDtypeStruct((field_count, bead_count, coef_width), jnp.float32),
+            jax.ShapeDtypeStruct((8, 128), jnp.float32),
+        ),
+        in_specs=[vmem] * 8,
+        out_specs=(vmem, vmem),
+        scratch_shapes=[
+            pltpu.VMEM(blocks, jnp.bfloat16),
+            pltpu.VMEM(blocks, jnp.bfloat16),
+            pltpu.VMEM((9, bead_count, 128), jnp.float32),
+            pltpu.VMEM((9, bead_count, wave_count), jnp.float32),
+            pltpu.VMEM((9, bead_count, wave_count), jnp.float32),
+            pltpu.VMEM((9, bead_count, 2 * bead_count), jnp.bfloat16),
+            pltpu.VMEM((field_count, 2 * bead_count, 2 * wave_count), jnp.float32),
+            pltpu.VMEM((nx, 8, 128), jnp.float32),
+            pltpu.VMEM((ny, 8, 128), jnp.float32),
+            dma((8, 1)),
+            dma((9, 1)),
+            dma((8, CHUNKS)),
+            dma((9, CHUNKS)),
+            dma((8, CHUNKS)),
+            dma((9, CHUNKS)),
+            dma((nx,)),
+            dma((nx,)),
+            dma((ny,)),
+            dma((ny,)),
+        ],
+        compiler_params=pltpu.CompilerParams(
+            collective_id=0, has_side_effects=True, vmem_limit_bytes=40 * 1024 * 1024
+        ),
+        name="krylov",
+    )(source, column_pos, row_pos, times, dirs, forward_matrix, back_matrix, mie_rows)
+    w_source, w_once = weights(gram[:, :field_count])
     answer = w_source[:, None, None] * source + w_once[:, None, None] * once
 
     cluster_dirs = sphere_grid(CLUSTER_LAT, CLUSTER_LON)

time: 152 us -> 111 us (0.73)
  Pallas kernels: 0 us -> 67.7 us
  blocking collectives: 39.9 us -> 0 us
  starting transfers between devices: 37.1 us -> 5.35 us
  waiting for transfers between devices: 30.9 us -> 2.3 us
  matrix products: 14.4 us -> 9.4 us
  other arithmetic: 12.4 us -> 10.1 us
    pallas_call x0 -> x1, Pallas kernels: none -> 67.7 us  [local(): pl.pallas_call(functools.partial(krylov_kernel, nx, ny), out_shape=(jax.S...]
    psum x1 -> x0, blocking collectives: 39.9 us -> none  [local(): gram = lax.psum(gram, ('gx', 'gy'))]
    ppermute x14 -> x2, starting transfers between devices: 37.1 us -> 5.35 us  [shift(): return lax.ppermute(block, axis, route)]
    ppermute x14 -> x2, waiting for transfers between devices: 30.9 us -> 2.3 us  [shift(): return lax.ppermute(block, axis, route)]
    dot_general x6 -> x0, matrix products: 5.68 us -> none  [the longest x2 2.74 us: scatter(): jnp.einsum('fnc,cq->fnq', blocks, forward_matrix, preferred_element_type=...]
    another operation x9 -> x3, other arithmetic: 3.66 us -> 0.1 us  [the longest x2 0.09 us: local(): jnp.stack([jnp.concatenate([mie[0], mie[0]]), jnp.concatenate([-mie[1], m...]
    neg x3, other arithmetic: 0.03 us -> 1.65 us  [block_matrix(): lower_half = jnp.concatenate([-pair[1], pair[0]], axis=1)]
    unnamed x61 -> x14, local copies, waits for them, and re-layouts: 3.43 us -> 2.38 us
  transfers between devices with their start and end apart: 14 -> 2, of which waited for: 10 -> 1; matrix products, arithmetic and copies ran while one was open for 10% -> 7% of each run, Pallas kernels for 0% -> 0%
where the time goes in v2:
time: 111 us; the launch traced here: 109 us
  Pallas kernels  67.7 us (61%)
  local copies, waits for them, and re-layouts  13.5 us (12%)
  other arithmetic  10.1 us (9%)
  matrix products  9.4 us (8%)
  starting transfers between devices  5.35 us (5%)
  waiting for transfers between devices  2.3 us (2%)
    pallas_call x1, Pallas kernels, local(): pl.pallas_call(functools.partial(krylov_kernel, nx, ny), out_shape=(jax.S...  67.7 us
    slice x1, local copies, waits for them, and re-layouts, local(): by_imag = jnp.dot(halves, cluster_waves[1], precision=HI)  6.69 us
    ppermute x2, starting transfers between devices, shift(): return lax.ppermute(block, axis, route)  5.35 us
    dot_general x1, matrix products, local(): jnp.einsum('fbc,cq->fbq', answer, block_matrix(to_cluster), precision=HI)  3.47 us
    reduce_sum x1, other arithmetic, local(): jnp.sum((flat_index[:, None, :] == rows[None, :, None]).astype(jnp.float3...  2.41 us
    unnamed x14, local copies, waits for them, and re-layouts  2.38 us
    ppermute x2, waiting for transfers between devices, shift(): return lax.ppermute(block, axis, route)  2.3 us
  transfers between devices with their start and end apart: 2, of which 1 were waited for; matrix products, arithmetic and copies ran while one was open for 7% of the time, Pallas kernels for 0%

profile of v2, /device:TPU:10, one launch (start us, length us, event | category | flops | bytes accessed | tf_op | source)
XLA Modules:
  0.0 109.2 jit_solution(4427952870776295537)
XLA Ops:
  0.8 0.7 fusion.54
  1.5 0.8 slice_bitcast_fusion.8
  2.3 0.7 fusion.55
  3.1 0.7 slice_bitcast_fusion.2
  3.8 0.9 fusion.56
  4.7 1.0 slice_bitcast_fusion
  5.7 0.7 copy.71
  6.4 0.9 fusion.6
  8.0 0.1 cosine_multiply_fusion
  8.3 0.8 multiply_add_fusion.3
  9.1 0.7 fusion.18
  9.9 0.7 fusion.65
  10.9 2.4 %convert_reduce_fusion = f32[576,128]{1,0:T(8,128)S(1)} fusion(s32[60,128]{1,0:T(8,128)S(1)} %pad_add_fusion), kind=kLoop, calls=%fused_computation | loop fusion | flops 13197312 | bytes 325632 | tf_op jit(solution)/shard_map/reduce_sum | solution.py:404
  13.4 0.2 copy.68
  13.6 0.2 multiply_subtract_fusion.1
  13.9 0.2 pad_maximum_fusion.source
  14.2 67.7 %krylov.1 = (f32[16,64,128]{2,1,0:T(8,128)S(1)}, f32[8,128]{1,0:T(8,128)S(1)}) custom-call(f32[16,64,128]{2,1,0:T(8,128)S(1)} %pad_maximum_fusion.source, f32[64,128]{1,0:T(8,128)S(1)} %pad.15.clone.column_pos, f32[8,128]{1,0:T(8,128)S(1)} %select_maximum_fusion.3.row_pos, f32[9,64,128]{2,1,0:T(8,128)S(1)} %bitcast.228, ...), custom_call_target="tpu_custom_call" | custom-call | tf_op jit(solution)/shard_map/krylov/pallas_call | solution.py:417
  82.1 0.6 fusion.16
  82.7 3.5 %fusion.7 = f32[16,64,1024]{2,1,0:T(8,128)S(1)} fusion(f32[64,512]{1,0:T(8,128)S(1)} %get-tuple-element.31, f32[64,512]{1,0:T(8,128)S(1)} %fusion.56, f32[64,512]{1,0:T(8,128)S(1)} %get-tuple-element.30, f32[16,64,128]{2,1,0:T(8,128)S(1)} %get-tuple-element.5, f32[16,64,128]{2,1,0:T(8,128)S(1)} %pad_maximum_fusion.source, f32[16]{0:T(128)S(1)} %mul.852, ...), kind=kOutput, calls=%fused_computation.16 | convolution fusion | flops 1611399168 | bytes 5636224 | tf_op jit(solution)/shard_map/fbc,cq->fbq/dot_general | solution.py:455
  86.1 0.8 multiply_subtract_fusion
  86.9 1.5 %fusion = f32[4,16,1024]{2,0,1:T(4,128)S(1)} fusion(f32[16,64,512]{2,1,0:T(8,128)S(1)} %get-tuple-element.21, f32[16,64,512]{2,1,0:T(8,128)S(1)} %get-tuple-element.20, s32[64]{0:T(128)S(1)} %fusion.26), kind=kOutput, calls=%fused_computation.2 | convolution fusion | flops 51380480 | bytes 4456704 | tf_op jit(solution)/shard_map/kb,fbq->kfq/dot_general | solution.py:469
  88.4 0.2 reshape.605
  88.6 0.2 fusion.62
  88.9 3.4 %collective-permute-start = (f32[2,16,1024]{2,0,1:T(2,128)S(1)}, f32[2,16,1024]{2,0,1:T(2,128)S(1)}, u32[]{:S(2)}, u32[]{:S(2)}) collective-permute-start(f32[2,16,1024]{2,0,1:T(2,128)S(1)} %bitcast.232), channel_id=1, source_target_pairs={{0,1},{1,2},{2,3},{3,4},{4,5},{5,6},{6,7},{8,9},{9,10},{10,11},{11... | collective-permute-start | bytes 393224 | tf_op jit(solution)/shard_map/ppermute | solution.py:23
  92.3 6.7 %fusion.61 = (f32[1,512,961]{1,0,2:T(1,128)S(1)}, f32[1,512,961]{1,0,2:T(1,128)S(1)}) fusion(f32[2,512,961]{1,0,2:T(2,128)} %param.22), kind=kLoop, calls=%fused_computation.149 | loop fusion | bytes 7872512 | tf_op jit(solution)/shard_map/slice | solution.py:476
  99.3 1.9 %collective-permute-start.1 = (f32[16,1024]{1,0:T(8,128)S(1)}, f32[16,1024]{1,0:T(8,128)S(1)}, u32[]{:S(2)}, u32[]{:S(2)}) collective-permute-start(f32[16,1024]{1,0:T(8,128)S(1)} %bitcast.233), channel_id=1, source_target_pairs={{0,8},{8,16},{16,24},{1,9},{9,17},{17,25},{2,10},{10,18},{18,26},{... | collective-permute-start | bytes 196616 | tf_op jit(solution)/shard_map/ppermute | solution.py:23
  101.2 0.3 fusion.57
  101.5 1.1 %copy.38 = f32[1,1,64,16,128]{4,3,2,1,0:T(8,128)} copy(f32[1,1,64,16,128]{4,2,3,1,0:T(8,128)S(1)} %fusion.57) | data formatting | bytes 1048576
  102.6 2.3 %collective-permute-done.1 = f32[16,1024]{1,0:T(8,128)S(1)} collective-permute-done((f32[16,1024]{1,0:T(8,128)S(1)}, f32[16,1024]{1,0:T(8,128)S(1)}, u32[]{:S(2)}, u32[]{:S(2)}) %collective-permute-start.1) | collective-permute-done | bytes 65568 | tf_op jit(solution)/shard_map/ppermute | solution.py:23
  104.9 1.8 %fusion.4 = f32[32,961]{1,0:T(8,128)S(1)} fusion(f32[1,512,961]{1,0,2:T(1,128)S(1)} %get-tuple-element.22, f32[16,512]{1,0:T(8,128)S(1)} %get-tuple-element.35, f32[16,512]{1,0:T(8,128)S(1)} %get-tuple-element.34), kind=kOutput, calls=%fused_computation.9 | convolution fusion | flops 188956672 | bytes 2156672 | tf_op jit(solution)/shard_map/dot_general | solution.py:476
  106.7 1.8 %fusion.5 = f32[32,961]{1,0:T(8,128)S(1)} fusion(f32[1,512,961]{1,0,2:T(1,128)S(1)} %get-tuple-element.23, f32[16,512]{1,0:T(8,128)S(1)} %get-tuple-element.35, f32[16,512]{1,0:T(8,128)S(1)} %get-tuple-element.34), kind=kOutput, calls=%fused_computation.11 | convolution fusion | flops 188956672 | bytes 2156672 | tf_op jit(solution)/shard_map/dot_general | solution.py:475
  108.5 0.7 maximum_bitcast_fusion.2
  (44 shorter events, 2.1 us)
Async XLA Ops:
  0.6 5.8 %copy-start = (f32[32,3]{0,1:T(4,128)S(1)}, f32[32,3]{0,1:T(4,128)}, u32[]{:S(2)}) copy-start(f32[32,3]{0,1:T(4,128)} %param.23) | copy-start | bytes 1156
  0.6 12.7 %copy-start.1 = (f32[1,1,64,16,128]{4,3,2,1,0:T(8,128)S(1)}, f32[1,1,64,16,128]{4,3,2,1,0:T(8,128)}, u32[]{:S(2)}) copy-start(f32[1,1,64,16,128]{4,3,2,1,0:T(8,128)} %param.12) | copy-start | bytes 1572868
  13.6 68.5 %copy-start.2 = (s32[1,1,64]{2,1,0:T(1,128)S(1)}, s32[1,1,64]{2,1,0:T(1,128)}, u32[]{:S(2)}) copy-start(s32[1,1,64]{2,1,0:T(1,128)} %param.17) | copy-start | bytes 772
  88.9 10.1 %collective-permute-start = (f32[2,16,1024]{2,0,1:T(2,128)S(1)}, f32[2,16,1024]{2,0,1:T(2,128)S(1)}, u32[]{:S(2)}, u32[]{:S(2)}) collective-permute-start(f32[2,16,1024]{2,0,1:T(2,128)S(1)} %bitcast.232), channel_id=1, source_target_pairs={{0,1},{1,2},{2,3},{3,4},{4,5},{5,6},{6,7},{8,9},{9,10},{10,11},{11... | collective-permute-start | bytes 393224 | tf_op jit(solution)/shard_map/ppermute | solution.py:23
  99.3 5.6 %collective-permute-start.1 = (f32[16,1024]{1,0:T(8,128)S(1)}, f32[16,1024]{1,0:T(8,128)S(1)}, u32[]{:S(2)}, u32[]{:S(2)}) collective-permute-start(f32[16,1024]{1,0:T(8,128)S(1)} %bitcast.233), channel_id=1, source_target_pairs={{0,8},{8,16},{16,24},{1,9},{9,17},{17,25},{2,10},{10,18},{18,26},{... | collective-permute-start | bytes 196616 | tf_op jit(solution)/shard_map/ppermute | solution.py:23

commit v3 on v2

--- a/solution.py
+++ b/solution.py
@@ -14,13 +14,6 @@
 CLUSTER_LON = 32
 WAVENUMBER = 3.0
 EPS = 1e-06
-HI = lax.Precision.HIGHEST
-
-
-def shift(block, axis, distance):
-    count = lax.axis_size(axis)
-    route = [(i - distance, i) for i in range(count) if 0 <= i - distance < count]
-    return lax.ppermute(block, axis, route)
 
 
 def sphere_grid(cycle_count, cycle_size):
@@ -53,11 +46,6 @@
         [real_part * cos_part - imag_part * sin_part, real_part * sin_part + imag_part * cos_part],
         axis=-1,
     )
-
-
-def angles(pos, dirs):
-    along = pos[0][:, None] * dirs[0] + pos[1][:, None] * dirs[1] + pos[2][:, None] * dirs[2]
-    return WAVENUMBER * along
 
 
 def weights(gram):
@@ -102,15 +90,34 @@
     forward_matrix,
     back_matrix,
     mie_rows,
+    to_cluster,
+    cluster_dirs,
+    cluster_waves,
+    answer,
+    expansion,
     once,
-    gram_out,
     buf_one,
     buf_two,
     geo,
     turn_cos,
     turn_sin,
     weight,
+    weight_rows,
     total,
+    tc_high,
+    tc_low,
+    cl_cos,
+    cl_sin,
+    cl_samples,
+    parts,
+    weight_cols,
+    waves,
+    waves_high,
+    waves_low,
+    cl_send,
+    cl_from_y,
+    cl_forward,
+    cl_from_x,
     gram_x,
     gram_y,
     geo_send,
@@ -123,11 +130,30 @@
     x_recv,
     y_send,
     y_recv,
+    waves_sem,
+    cl_sems,
 ):
     i, j = lax.axis_index("gx"), lax.axis_index("gy")
     fields, beads, width = source.shape
     wide = turn_cos.shape[2]
     step = fields // CHUNKS
+    waves_copy = pltpu.make_async_copy(cluster_waves, waves, waves_sem)
+    waves_copy.start()
+
+    def loop(first, last, body, carry, size=4):
+        def several(k, carry):
+            for u in range(size):
+                carry = body(first + k * size + u, carry)
+            return carry
+
+        return lax.fori_loop(0, (last - first) // size, several, carry)
+
+    def split(value):
+        high = value.astype(jnp.bfloat16)
+        return high, (value - high.astype(jnp.float32)).astype(jnp.bfloat16)
+
+    def dot(a, b):
+        return jnp.dot(a, b, preferred_element_type=jnp.float32)
 
     def present(dx, dy):
         return (i + dx >= 0) & (i + dx < nx) & (j + dy >= 0) & (j + dy < ny)
@@ -251,16 +277,66 @@
         full = times[p] / (1.0 + dist)
         high = full.astype(jnp.bfloat16).astype(jnp.float32)
         lane = lax.broadcasted_iota(jnp.int32, full.shape, 1)
-        weight[p] = jnp.where(lane < beads, high, full - high).astype(jnp.bfloat16)
+        weight_rows[p] = jnp.where(lane < beads, high, full - high)
+
+    def turn_weights(g):
+        rows = weight_rows[3 * g : 3 * g + 3].reshape(3 * beads, 2 * beads)
+        weight[g] = jnp.transpose(rows).astype(jnp.bfloat16)
+
+    cl_wide = cl_cos.shape[1]
+
+    def cluster_setup():
+        along = (
+            column_pos[:, 3:4] * cluster_dirs[0:1, :]
+            + column_pos[:, 4:5] * cluster_dirs[1:2, :]
+            + column_pos[:, 5:6] * cluster_dirs[2:3, :]
+        )
+        angle = WAVENUMBER * along
+        cl_cos[...] = jnp.cos(angle)
+        cl_sin[...] = jnp.sin(angle)
+        half = width // 2
+        real_high, real_low = split(to_cluster[0])
+        imag_high, imag_low = split(to_cluster[1])
+        for ref, real, imag in ((tc_high, real_high, imag_high), (tc_low, real_low, imag_low)):
+            ref[0:half, 0:cl_wide] = real
+            ref[0:half, cl_wide : 2 * cl_wide] = imag
+            ref[half:width, 0:cl_wide] = -imag
+            ref[half:width, cl_wide : 2 * cl_wide] = real
+
+    def cluster_parts(values, kind, c):
+        high, low = split(values[pl.ds(c * step, step)].reshape(step * beads, width))
+        smp = dot(high, tc_high[...]) + dot(low, tc_high[...]) + dot(high, tc_low[...])
+        cl_samples[...] = smp.reshape(step, beads, 2 * cl_wide)
+
+        def body(f, carry):
+            re, im = cl_samples[f, :, :cl_wide], cl_samples[f, :, cl_wide:]
+            co, si = cl_cos[...], cl_sin[...]
+            real = re * co - im * si
+            imag = re * si + im * co
+            for k in range(4):
+                hot = column_pos[:, 8 + k : 9 + k]
+                spot = pl.ds(c * step + f, 1)
+                parts[kind, k, spot, 0:cl_wide] = jnp.sum(real * hot, axis=0, keepdims=True)
+                parts[kind, k, spot, cl_wide : 2 * cl_wide] = jnp.sum(
+                    imag * hot, axis=0, keepdims=True
+                )
+            return carry
+
+        lax.fori_loop(0, step, body, 0)
 
     geometry(4)
     for p in (3, 5):
         geometry(p)
+    turn_weights(1)
+    cluster_setup()
     for c in range(CHUNKS):
         forward(one_group, c)
+        cluster_parts(source, 0, c)
     for p in (0, 1, 2, 6, 7, 8):
         arrive(geo_group, p, 0)
         geometry(p)
+    turn_weights(0)
+    turn_weights(2)
 
     def gathered(buf, f, first, count):
         rows = count * beads
@@ -277,12 +353,7 @@
             ],
             axis=1,
         )
-        return lax.dot_general(
-            weight[spot].reshape(rows, 2 * beads),
-            turned,
-            (((0,), (0,)), ((), ())),
-            preferred_element_type=jnp.float32,
-        )
+        return dot(weight[first // 3], turned)
 
     def back_turn(acc):
         inc = acc[:beads] + acc[beads:]
@@ -304,7 +375,7 @@
             total[f] = gathered(buf, f, 3, 3)
             return carry
 
-        lax.fori_loop(0, fields, body, 0)
+        loop(0, fields, body, 0)
 
     def sides(buf, f):
         return back_turn(total[f] + gathered(buf, f, 0, 3) + gathered(buf, f, 6, 3))
@@ -320,12 +391,24 @@
             buf_two[f, 4] = value.astype(jnp.bfloat16)
             return carry
 
-        lax.fori_loop(c * step, (c + 1) * step, first, 0)
+        loop(c * step, (c + 1) * step, first, 0)
         start(two_group, own_routes, c)
 
     for c in range(CHUNKS):
+        cluster_parts(once, 1, c)
         forward(two_group, c)
     middle(buf_two)
+    waves_copy.wait()
+
+    def halve(k, carry):
+        spot = pl.ds(k * 64, 64)
+        for part in range(2):
+            high, low = split(waves[part, spot, :])
+            waves_high[part, spot, :] = high
+            waves_low[part, spot, :] = low
+        return carry
+
+    lax.fori_loop(0, waves.shape[1] // 64, halve, 0)
 
     row = lax.broadcasted_iota(jnp.int32, (8, 128), 0)
     lane = lax.broadcasted_iota(jnp.int32, (8, 128), 1)
@@ -342,7 +425,7 @@
                 gram = gram + jnp.where((row == k) & (lane == f), value, 0.0)
             return gram
 
-        gram = lax.fori_loop(c * step, (c + 1) * step, second, gram)
+        gram = loop(c * step, (c + 1) * step, second, gram, 2)
 
     def reduce_over(gram, slots, send, recv, count, peer):
         slots[0] = gram
@@ -367,7 +450,81 @@
 
     gram = reduce_over(gram, gram_x, x_send, x_recv, nx, lambda d: (lax.rem(i + d, nx), j))
     gram = reduce_over(gram, gram_y, y_send, y_recv, ny, lambda d: (i, lax.rem(j + d, ny)))
-    gram_out[...] = gram
+    w_source, w_once = weights([gram[k : k + 1] for k in range(6)])
+    diagonal = lax.broadcasted_iota(jnp.int32, (fields, 128), 0) == lax.broadcasted_iota(
+        jnp.int32, (fields, 128), 1
+    )
+    columns = []
+    for k, w in enumerate((w_source, w_once)):
+        column = jnp.sum(jnp.where(diagonal, w, 0.0), axis=1, keepdims=True)
+        columns.append(column)
+        weight_cols[k] = jnp.broadcast_to(column, (fields, 128))
+    mixed = [parts[0, k] * columns[0] + parts[1, k] * columns[1] for k in range(4)]
+    cl_send[0] = mixed[1]
+    cl_send[1] = mixed[3]
+
+    def move(src, dst, base, dx, dy):
+        return pltpu.make_async_remote_copy(
+            src_ref=src,
+            dst_ref=dst,
+            send_sem=cl_sems.at[base],
+            recv_sem=cl_sems.at[base + 1],
+            device_id=(i + dx, j + dy),
+            device_id_type=pl.DeviceIdType.MESH,
+        )
+
+    @pl.when(j < ny - 1)
+    def _():
+        move(cl_send, cl_from_y, 0, 0, 1).start()
+
+    @pl.when(j == 0)
+    def _():
+        cl_from_y[...] = jnp.zeros(cl_from_y.shape, jnp.float32)
+
+    @pl.when(i == 0)
+    def _():
+        cl_from_x[...] = jnp.zeros(cl_from_x.shape, jnp.float32)
+
+    @pl.when(j > 0)
+    def _():
+        move(cl_send, cl_from_y, 0, 0, -1).wait_recv()
+
+    cl_forward[...] = mixed[2] + cl_from_y[1]
+
+    @pl.when(i < nx - 1)
+    def _():
+        move(cl_forward, cl_from_x, 2, 1, 0).start()
+
+    def combine(f, carry):
+        ws = weight_cols[0, pl.ds(f, 1), :]
+        wo = weight_cols[1, pl.ds(f, 1), :]
+        answer[f] = source[f] * ws + once[f] * wo
+        return carry
+
+    lax.fori_loop(0, fields, combine, 0)
+
+    @pl.when(i > 0)
+    def _():
+        move(cl_forward, cl_from_x, 2, -1, 0).wait_recv()
+
+    own = mixed[0] + cl_from_y[0] + cl_from_x[...]
+    halves = jnp.concatenate([own[:, :cl_wide], own[:, cl_wide:]], axis=0)
+    high, low = split(halves)
+    by = [
+        dot(high, waves_high[k]) + dot(low, waves_high[k]) + dot(high, waves_low[k])
+        for k in range(2)
+    ]
+    expansion[0] = by[0][:fields] - by[1][fields:]
+    expansion[1] = by[1][:fields] + by[0][fields:]
+
+    @pl.when(j < ny - 1)
+    def _():
+        move(cl_send, cl_from_y, 0, 0, 1).wait_send()
+
+    @pl.when(i < nx - 1)
+    def _():
+        move(cl_forward, cl_from_x, 2, 1, 0).wait_send()
+
     finish_sends(geo_group, 1)
     finish_sends(one_group, CHUNKS)
     finish_sends(two_group, CHUNKS)
@@ -404,7 +561,25 @@
     times = jnp.sum((flat_index[:, None, :] == rows[None, :, None]).astype(jnp.float32), axis=0)
     times = times.reshape(9, bead_count, 2 * bead_count)
     dirs = jnp.pad(sphere_grid(WAVE_LAT, WAVE_LON), ((0, 5), (0, 0)))
-    column_pos = jnp.pad(jnp.transpose(own_pos), ((0, 0), (0, 125)))
+    bead_ids = cluster_id[0, 0]
+    cluster_total = centers.shape[0]
+    one_hot = (bead_ids[:, None] == jnp.arange(cluster_total, dtype=jnp.int32)[None, :]).astype(
+        jnp.float32
+    )
+    bead_centre = jnp.sum(one_hot[:, :, None] * centers[None], axis=1)
+    span_y = lax.axis_size("gy")
+    code = (bead_ids // span_y - lax.axis_index("gx")) * 2 + (
+        bead_ids % span_y - lax.axis_index("gy")
+    )
+    hot = (code[:, None] == jnp.arange(4, dtype=jnp.int32)[None, :]).astype(jnp.float32)
+    pos_t = jnp.transpose(own_pos)
+    column_pos = jnp.concatenate(
+        [pos_t, pos_t - bead_centre, jnp.zeros((bead_count, 2), jnp.float32), hot], axis=1
+    )
+    column_pos = jnp.pad(column_pos, ((0, 0), (0, 116)))
+    cluster_dirs = jnp.pad(sphere_grid(CLUSTER_LAT, CLUSTER_LON), ((0, 5), (0, 0)))
+    cl_wide = to_cluster.shape[2]
+    cl_coef = cluster_waves.shape[2]
     row_pos = jnp.pad(jnp.concatenate([own_pos, own_pos], axis=1), ((0, 5), (0, 0)))
     mie_rows = jnp.stack(
         [jnp.concatenate([mie[0], mie[0]]), jnp.concatenate([-mie[1], mie[1]])]
@@ -414,22 +589,38 @@
     vmem = pl.BlockSpec(memory_space=pltpu.VMEM)
     dma = pltpu.SemaphoreType.DMA
     blocks = (field_count, 9, bead_count, coef_width)
-    once, gram = pl.pallas_call(
+    answer, expansion = pl.pallas_call(
         functools.partial(krylov_kernel, nx, ny),
         out_shape=(
             jax.ShapeDtypeStruct((field_count, bead_count, coef_width), jnp.float32),
-            jax.ShapeDtypeStruct((8, 128), jnp.float32),
+            jax.ShapeDtypeStruct((2, field_count, cl_coef), jnp.float32),
         ),
-        in_specs=[vmem] * 8,
+        in_specs=[vmem] * 10 + [pl.BlockSpec(memory_space=pl.ANY)],
         out_specs=(vmem, vmem),
         scratch_shapes=[
+            pltpu.VMEM((field_count, bead_count, coef_width), jnp.float32),
             pltpu.VMEM(blocks, jnp.bfloat16),
             pltpu.VMEM(blocks, jnp.bfloat16),
             pltpu.VMEM((9, bead_count, 128), jnp.float32),
             pltpu.VMEM((9, bead_count, wave_count), jnp.float32),
             pltpu.VMEM((9, bead_count, wave_count), jnp.float32),
-            pltpu.VMEM((9, bead_count, 2 * bead_count), jnp.bfloat16),
+            pltpu.VMEM((3, 2 * bead_count, 3 * bead_count), jnp.bfloat16),
+            pltpu.VMEM((9, bead_count, 2 * bead_count), jnp.float32),
             pltpu.VMEM((field_count, 2 * bead_count, 2 * wave_count), jnp.float32),
+            pltpu.VMEM((coef_width, 2 * cl_wide), jnp.bfloat16),
+            pltpu.VMEM((coef_width, 2 * cl_wide), jnp.bfloat16),
+            pltpu.VMEM((bead_count, cl_wide), jnp.float32),
+            pltpu.VMEM((bead_count, cl_wide), jnp.float32),
+            pltpu.VMEM((field_count // CHUNKS, bead_count, 2 * cl_wide), jnp.float32),
+            pltpu.VMEM((2, 4, field_count, 2 * cl_wide), jnp.float32),
+            pltpu.VMEM((2, field_count, 128), jnp.float32),
+            pltpu.VMEM(cluster_waves.shape, jnp.float32),
+            pltpu.VMEM(cluster_waves.shape, jnp.bfloat16),
+            pltpu.VMEM(cluster_waves.shape, jnp.bfloat16),
+            pltpu.VMEM((2, field_count, 2 * cl_wide), jnp.float32),
+            pltpu.VMEM((2, field_count, 2 * cl_wide), jnp.float32),
+            pltpu.VMEM((field_count, 2 * cl_wide), jnp.float32),
+            pltpu.VMEM((field_count, 2 * cl_wide), jnp.float32),
             pltpu.VMEM((nx, 8, 128), jnp.float32),
             pltpu.VMEM((ny, 8, 128), jnp.float32),
             dma((8, 1)),
@@ -442,45 +633,27 @@
             dma((nx,)),
             dma((ny,)),
             dma((ny,)),
+            dma,
+            dma((4,)),
         ],
         compiler_params=pltpu.CompilerParams(
             collective_id=0, has_side_effects=True, vmem_limit_bytes=40 * 1024 * 1024
         ),
         name="krylov",
-    )(source, column_pos, row_pos, times, dirs, forward_matrix, back_matrix, mie_rows)
-    w_source, w_once = weights(gram[:, :field_count])
-    answer = w_source[:, None, None] * source + w_once[:, None, None] * once
-
-    cluster_dirs = sphere_grid(CLUSTER_LAT, CLUSTER_LON)
-    samples = jnp.einsum("fbc,cq->fbq", answer, block_matrix(to_cluster), precision=HI)
-    bead_ids = cluster_id[0, 0]
-    cluster_total = centers.shape[0]
-    one_hot = (bead_ids[:, None] == jnp.arange(cluster_total, dtype=jnp.int32)[None, :]).astype(
-        jnp.float32
-    )
-    bead_centre = jnp.dot(one_hot, centers, precision=HI)
-    turn = angles(own_pos - jnp.transpose(bead_centre), cluster_dirs)
-    shifted = times_phase(samples, jnp.cos(turn), jnp.sin(turn))
-    span_y = lax.axis_size("gy")
-    code = (bead_ids // span_y - lax.axis_index("gx")) * 2 + (
-        bead_ids % span_y - lax.axis_index("gy")
-    )
-    hot = (jnp.arange(4, dtype=jnp.int32)[:, None] == code[None, :]).astype(jnp.float32)
-    part = jnp.einsum("kb,fbq->kfq", hot, shifted, precision=HI)
-    part = part.reshape(2, 2, field_count, -1)
-    section = part[:, 0] + shift(part[:, 1], "gy", 1)
-    own = section[0] + shift(section[1], "gx", 1)
-    half = own.shape[1] // 2
-    halves = jnp.concatenate([own[:, :half], own[:, half:]], axis=0)
-    by_real = jnp.dot(halves, cluster_waves[0], precision=HI)
-    by_imag = jnp.dot(halves, cluster_waves[1], precision=HI)
-    expansions = jnp.concatenate(
-        [
-            by_real[:field_count] - by_imag[field_count:],
-            by_imag[:field_count] + by_real[field_count:],
-        ],
-        axis=1,
-    )
+    )(
+        source,
+        column_pos,
+        row_pos,
+        times,
+        dirs,
+        forward_matrix,
+        back_matrix,
+        mie_rows,
+        to_cluster,
+        cluster_dirs,
+        cluster_waves,
+    )
+    expansions = jnp.concatenate([expansion[0], expansion[1]], axis=1)
     return (jnp.transpose(answer, (1, 0, 2))[None, None], expansions[None])
 
 

time: 111 us -> 98.6 us (0.89)
  matrix products: 9.4 us -> 0 us
  starting transfers between devices: 5.35 us -> 0 us
  Pallas kernels: 67.7 us -> 70.2 us
  local copies, waits for them, and re-layouts: 13.5 us -> 15.8 us
  waiting for transfers between devices: 2.3 us -> 0 us
    unnamed x14 -> x10, local copies, waits for them, and re-layouts: 2.38 us -> 12.8 us
    dot_general x5 -> x0, matrix products: 9.4 us -> none  [the longest x1 3.47 us: local(): jnp.einsum('fbc,cq->fbq', answer, block_matrix(to_cluster), precision=HI)]
    slice x4 -> x0, local copies, waits for them, and re-layouts: 7 us -> none  [the longest x1 6.69 us: local(): by_imag = jnp.dot(halves, cluster_waves[1], precision=HI)]
    ppermute x2 -> x0, starting transfers between devices: 5.35 us -> none  [shift(): return lax.ppermute(block, axis, route)]
    pallas_call x1, Pallas kernels: 67.7 us -> 70.2 us  [local(): pl.pallas_call(functools.partial(krylov_kernel, nx, ny), out_shape=(jax.S...]
    ppermute x2 -> x0, waiting for transfers between devices: 2.3 us -> none  [shift(): return lax.ppermute(block, axis, route)]
  transfers between devices with their start and end apart: 2 -> 0, of which waited for: 1 -> 0; matrix products, arithmetic and copies ran while one was open for 7% -> 0% of each run, Pallas kernels for 0% -> 0%
where the time goes in v3:
time: 98.6 us; the launch traced here: 96.9 us
  Pallas kernels  70.2 us (71%)
  local copies, waits for them, and re-layouts  15.8 us (16%)
  other arithmetic  10.1 us (10%)
    pallas_call x1, Pallas kernels, local(): pl.pallas_call(functools.partial(krylov_kernel, nx, ny), out_shape=(jax.S...  70.2 us
    unnamed x10, local copies, waits for them, and re-layouts  12.8 us
    reduce_sum x1, other arithmetic, local(): jnp.sum((flat_index[:, None, :] == rows[None, :, None]).astype(jnp.float3...  2.4 us

profile of v3, /device:TPU:10, one launch (start us, length us, event | category | flops | bytes accessed | tf_op | source)
XLA Modules:
  0.0 96.9 jit_solution(17486730091339942668)
XLA Ops:
  0.6 0.7 fusion.4
  1.3 0.7 fusion.14
  2.2 0.8 slice_bitcast_fusion.5
  3.1 0.7 copy.46
  3.9 0.1 stack_reshape.4
  4.0 0.1 cosine_multiply_fusion.1
  4.1 0.1 mul.251
  4.2 0.1 mul.253
  4.4 0.1 stack_reshape.5
  4.5 0.1 cosine_multiply_fusion
  4.8 0.7 fusion.1
  5.5 0.8 multiply_reduce_fusion
  6.2 0.7 fusion.13
  7.0 0.7 fusion.15
  7.7 0.1 copy.30
  7.8 0.8 multiply_add_fusion.1
  8.6 0.7 fusion
  9.3 0.1 pad_add_fusion
  9.4 0.7 fusion.16
  10.1 0.1 copy.38
  10.2 0.1 copy.37
  10.4 0.1 maximum_maximum_fusion.1.back_matrix
  10.5 0.7 slice_bitcast_fusion.2
  11.2 2.4 %convert_reduce_fusion = f32[576,128]{1,0:T(8,128)S(1)} fusion(s32[60,128]{1,0:T(8,128)S(1)} %pad_add_fusion), kind=kLoop, calls=%fused_computation | loop fusion | flops 13197312 | bytes 325632 | tf_op jit(solution)/shard_map/reduce_sum | solution.py:561
  13.6 1.2 %copy.45 = f32[1,1,64,16,128]{4,2,3,1,0:T(8,128)S(1)} copy(f32[1,1,64,16,128]{4,3,2,1,0:T(8,128)} %param.12) | data formatting | bytes 1048576 | tf_op args[0]
  14.8 0.2 multiply_subtract_fusion
  15.1 0.2 pad_maximum_fusion.source
  15.3 7.3 %copy.33.cluster_waves = f32[2,512,961]{2,1,0:T(8,128)} copy(f32[2,512,961]{1,0,2:T(2,128)} %param.22) | data formatting | bytes 7872512 | tf_op args[10]
  22.6 2.2 %copy-done = f32[2,512,961]{2,1,0:T(8,128)S(1)} copy-done((f32[2,512,961]{2,1,0:T(8,128)S(1)}, f32[2,512,961]{2,1,0:T(8,128)}, u32[]{:S(2)}) %copy-start) | copy-done | bytes 3936280
  24.8 70.2 %krylov.1 = (f32[16,64,128]{2,1,0:T(8,128)S(1)}, f32[2,16,961]{2,1,0:T(8,128)S(1)}) custom-call(f32[16,64,128]{2,1,0:T(8,128)S(1)} %pad_maximum_fusion.source, f32[64,128]{1,0:T(8,128)S(1)} %pad.19.column_pos, f32[8,128]{1,0:T(8,128)S(1)} %select_maximum_fusion.5.row_pos, f32[9,64,128]{2,1,0:T(8,128)S(1)} %bitcast.51, ...), custom_call_target="tpu_custom_call" | custom-call | tf_op jit(solution)/shard_map/krylov/pallas_call | solution.py:592
  95.0 1.1 %copy.34 = f32[1,1,64,16,128]{4,3,2,1,0:T(8,128)} copy(f32[1,1,64,16,128]{4,2,3,1,0:T(8,128)S(1)} %bitcast.52) | data formatting | bytes 1048576
  96.2 0.7 maximum_bitcast_fusion
  (24 shorter events, 0.9 us)
Async XLA Ops:
  15.3 7.4 %copy-start.1 = (f32[2,64,512]{2,1,0:T(8,128)S(1)}, f32[2,64,512]{2,1,0:T(8,128)}, u32[]{:S(2)}) copy-start(f32[2,64,512]{2,1,0:T(8,128)} %to_cluster.1) | copy-start | bytes 786436
  22.6 2.2 %copy-start = (f32[2,512,961]{2,1,0:T(8,128)S(1)}, f32[2,512,961]{2,1,0:T(8,128)}, u32[]{:S(2)}) copy-start(f32[2,512,961]{2,1,0:T(8,128)} %copy.33.cluster_waves) | copy-start | bytes 11808772

commit v4 on v3

--- a/solution.py
+++ b/solution.py
@@ -3,6 +3,7 @@
 
 import jax
 import jax.numpy as jnp
+import numpy as np
 from jax import lax
 from jax.experimental import pallas as pl
 from jax.experimental.pallas import tpu as pltpu
@@ -17,35 +18,16 @@
 
 
 def sphere_grid(cycle_count, cycle_size):
-    polar = (jnp.arange(cycle_count, dtype=jnp.float32) + 0.5) * (math.pi / cycle_count)
-    cycle_index = jnp.arange(cycle_size, dtype=jnp.float32)
-    stagger = 0.5 * (jnp.arange(cycle_count, dtype=jnp.int32) % 2).astype(jnp.float32)
-    azimuth = (cycle_index[None, :] + stagger[:, None]) * (2.0 * math.pi / cycle_size)
-    height = jnp.cos(polar)[:, None] * jnp.ones_like(azimuth)
-    radius = jnp.sin(polar)[:, None]
-    return jnp.stack(
-        [
-            (radius * jnp.cos(azimuth)).reshape(-1),
-            (radius * jnp.sin(azimuth)).reshape(-1),
-            height.reshape(-1),
-        ]
-    )
-
-
-def block_matrix(pair):
-    top_half = jnp.concatenate([pair[0], pair[1]], axis=1)
-    lower_half = jnp.concatenate([-pair[1], pair[0]], axis=1)
-    return jnp.concatenate([top_half, lower_half], axis=0)
-
-
-def times_phase(values, cos_part, sin_part):
-    half_width = values.shape[-1] // 2
-    real_part = values[..., :half_width]
-    imag_part = values[..., half_width:]
-    return jnp.concatenate(
-        [real_part * cos_part - imag_part * sin_part, real_part * sin_part + imag_part * cos_part],
-        axis=-1,
-    )
+    polar = (np.arange(cycle_count) + 0.5) * (math.pi / cycle_count)
+    stagger = 0.5 * (np.arange(cycle_count) % 2)
+    azimuth = (np.arange(cycle_size)[None, :] + stagger[:, None]) * (2.0 * math.pi / cycle_size)
+    height = np.cos(polar)[:, None] * np.ones_like(azimuth)
+    radius = np.sin(polar)[:, None]
+    grid = np.zeros((8, cycle_count * cycle_size), np.float32)
+    grid[0] = (radius * np.cos(azimuth)).reshape(-1)
+    grid[1] = (radius * np.sin(azimuth)).reshape(-1)
+    grid[2] = height.reshape(-1)
+    return grid
 
 
 def weights(gram):
@@ -82,19 +64,23 @@
 def krylov_kernel(
     nx,
     ny,
-    source,
+    incident,
     column_pos,
     row_pos,
     times,
     dirs,
-    forward_matrix,
-    back_matrix,
-    mie_rows,
+    to_waves,
+    from_waves,
+    mie,
     to_cluster,
     cluster_dirs,
     cluster_waves,
     answer,
     expansion,
+    source,
+    forward_matrix,
+    back_matrix,
+    mie_rows,
     once,
     buf_one,
     buf_two,
@@ -137,7 +123,8 @@
     fields, beads, width = source.shape
     wide = turn_cos.shape[2]
     step = fields // CHUNKS
-    waves_copy = pltpu.make_async_copy(cluster_waves, waves, waves_sem)
+    wave_rows = cluster_waves.shape[0]
+    waves_copy = pltpu.make_async_copy(cluster_waves, waves.at[pl.ds(0, wave_rows)], waves_sem)
     waves_copy.start()
 
     def loop(first, last, body, carry, size=4):
@@ -154,6 +141,11 @@
 
     def dot(a, b):
         return jnp.dot(a, b, preferred_element_type=jnp.float32)
+
+    def dot_turned(a, b):
+        return lax.dot_general(
+            a, b, (((1,), (1,)), ((), ())), preferred_element_type=jnp.float32
+        )
 
     def present(dx, dy):
         return (i + dx >= 0) & (i + dx < nx) & (j + dy >= 0) & (j + dy < ny)
@@ -237,11 +229,27 @@
         )
     geo[4] = column_pos[...]
 
-    def to_low(f, carry):
-        buf_one[f, 4] = source[f].astype(jnp.bfloat16)
-        return carry
-
-    lax.fori_loop(0, fields, to_low, 0)
+    half = width // 2
+    mie_rows[0:1, 0:half] = mie[0:1, :]
+    mie_rows[0:1, half:width] = mie[0:1, :]
+    mie_rows[1:2, 0:half] = -mie[1:2, :]
+    mie_rows[1:2, half:width] = mie[1:2, :]
+    for f in range(fields):
+        value = incident[:, f, :]
+        value = value * mie_rows[0:1, :] + pltpu.roll(value, half, 1) * mie_rows[1:2, :]
+        source[f] = value
+        buf_one[f, 4] = value.astype(jnp.bfloat16)
+    forward_matrix[0:half, 0:wide] = to_waves[0]
+    forward_matrix[0:half, wide : 2 * wide] = to_waves[1]
+    forward_matrix[half:width, 0:wide] = -to_waves[1]
+    forward_matrix[half:width, wide : 2 * wide] = to_waves[0]
+    back_matrix[0:half, 0:wide] = from_waves[0]
+    back_matrix[0:half, wide : 2 * wide] = -from_waves[1]
+    back_matrix[half:width, 0:wide] = from_waves[1]
+    back_matrix[half:width, wide : 2 * wide] = from_waves[0]
+    waves[pl.ds(wave_rows, waves.shape[0] - wave_rows)] = jnp.zeros(
+        (waves.shape[0] - wave_rows, 128), jnp.float32
+    )
     for p, (dx, dy) in enumerate(SHIFTS):
 
         @pl.when(jnp.logical_not(present(dx, dy)))
@@ -294,7 +302,6 @@
         angle = WAVENUMBER * along
         cl_cos[...] = jnp.cos(angle)
         cl_sin[...] = jnp.sin(angle)
-        half = width // 2
         real_high, real_low = split(to_cluster[0])
         imag_high, imag_low = split(to_cluster[1])
         for ref, real, imag in ((tc_high, real_high, imag_high), (tc_low, real_low, imag_low)):
@@ -362,11 +369,7 @@
         inc = jnp.concatenate([re * co - im * si, re * si + im * co], axis=1)
         high = inc.astype(jnp.bfloat16)
         low = (inc - high.astype(jnp.float32)).astype(jnp.bfloat16)
-        back = jnp.dot(
-            jnp.concatenate([high, low], axis=0),
-            back_matrix[...],
-            preferred_element_type=jnp.float32,
-        )
+        back = dot_turned(jnp.concatenate([high, low], axis=0), back_matrix[...])
         back = back[:beads] + back[beads:]
         return back * mie_rows[0:1, :] + pltpu.roll(back, width // 2, 1) * mie_rows[1:2, :]
 
@@ -400,15 +403,13 @@
     middle(buf_two)
     waves_copy.wait()
 
-    def halve(k, carry):
-        spot = pl.ds(k * 64, 64)
+    lanes = cl_wide // 128
+    for block in range(lanes):
         for part in range(2):
-            high, low = split(waves[part, spot, :])
-            waves_high[part, spot, :] = high
-            waves_low[part, spot, :] = low
-        return carry
-
-    lax.fori_loop(0, waves.shape[1] // 64, halve, 0)
+            rows = waves_high.shape[1]
+            high, low = split(waves[pl.ds(2 * block + part, rows, stride=2 * lanes), :])
+            waves_high[part, :, 128 * block : 128 * block + 128] = high
+            waves_low[part, :, 128 * block : 128 * block + 128] = low
 
     row = lax.broadcasted_iota(jnp.int32, (8, 128), 0)
     lane = lax.broadcasted_iota(jnp.int32, (8, 128), 1)
@@ -511,7 +512,9 @@
     halves = jnp.concatenate([own[:, :cl_wide], own[:, cl_wide:]], axis=0)
     high, low = split(halves)
     by = [
-        dot(high, waves_high[k]) + dot(low, waves_high[k]) + dot(high, waves_low[k])
+        dot_turned(high, waves_high[k])
+        + dot_turned(low, waves_high[k])
+        + dot_turned(high, waves_low[k])
         for k in range(2)
     ]
     expansion[0] = by[0][:fields] - by[1][fields:]
@@ -548,9 +551,6 @@
     field_count = incident.shape[3]
     coef_width = incident.shape[4]
     wave_count = to_waves.shape[2]
-    forward_matrix = block_matrix(to_waves)
-    back_matrix = block_matrix(from_waves)
-    source = times_phase(jnp.transpose(incident[0, 0], (1, 0, 2)), mie[0], mie[1])
     own_pos = positions[0, 0]
     flat_index = nbr_part[0, 0] * bead_count + nbr_slot[0, 0]
     slots = jnp.arange(flat_index.shape[1], dtype=jnp.int32)
@@ -560,7 +560,7 @@
     rows = jnp.arange(9 * bead_count, dtype=jnp.int32)
     times = jnp.sum((flat_index[:, None, :] == rows[None, :, None]).astype(jnp.float32), axis=0)
     times = times.reshape(9, bead_count, 2 * bead_count)
-    dirs = jnp.pad(sphere_grid(WAVE_LAT, WAVE_LON), ((0, 5), (0, 0)))
+    dirs = sphere_grid(WAVE_LAT, WAVE_LON)
     bead_ids = cluster_id[0, 0]
     cluster_total = centers.shape[0]
     one_hot = (bead_ids[:, None] == jnp.arange(cluster_total, dtype=jnp.int32)[None, :]).astype(
@@ -577,14 +577,14 @@
         [pos_t, pos_t - bead_centre, jnp.zeros((bead_count, 2), jnp.float32), hot], axis=1
     )
     column_pos = jnp.pad(column_pos, ((0, 0), (0, 116)))
-    cluster_dirs = jnp.pad(sphere_grid(CLUSTER_LAT, CLUSTER_LON), ((0, 5), (0, 0)))
+    cluster_dirs = sphere_grid(CLUSTER_LAT, CLUSTER_LON)
     cl_wide = to_cluster.shape[2]
     cl_coef = cluster_waves.shape[2]
+    lanes = cl_wide // 128
+    flat_waves = jnp.transpose(cluster_waves, (2, 0, 1)).reshape(cl_coef, 2, lanes, 128)
+    flat_waves = jnp.transpose(flat_waves, (0, 2, 1, 3)).reshape(cl_coef * 2 * lanes, 128)
+    cl_rows = -(-cl_coef // 16) * 16
     row_pos = jnp.pad(jnp.concatenate([own_pos, own_pos], axis=1), ((0, 5), (0, 0)))
-    mie_rows = jnp.stack(
-        [jnp.concatenate([mie[0], mie[0]]), jnp.concatenate([-mie[1], mie[1]])]
-    )
-    mie_rows = jnp.pad(mie_rows, ((0, 6), (0, 0)))
     nx, ny = lax.axis_size("gx"), lax.axis_size("gy")
     vmem = pl.BlockSpec(memory_space=pltpu.VMEM)
     dma = pltpu.SemaphoreType.DMA
@@ -593,11 +593,15 @@
         functools.partial(krylov_kernel, nx, ny),
         out_shape=(
             jax.ShapeDtypeStruct((field_count, bead_count, coef_width), jnp.float32),
-            jax.ShapeDtypeStruct((2, field_count, cl_coef), jnp.float32),
+            jax.ShapeDtypeStruct((2, field_count, cl_rows), jnp.float32),
         ),
         in_specs=[vmem] * 10 + [pl.BlockSpec(memory_space=pl.ANY)],
         out_specs=(vmem, vmem),
         scratch_shapes=[
+            pltpu.VMEM((field_count, bead_count, coef_width), jnp.float32),
+            pltpu.VMEM((coef_width, 2 * wave_count), jnp.bfloat16),
+            pltpu.VMEM((coef_width, 2 * wave_count), jnp.bfloat16),
+            pltpu.VMEM((8, coef_width), jnp.float32),
             pltpu.VMEM((field_count, bead_count, coef_width), jnp.float32),
             pltpu.VMEM(blocks, jnp.bfloat16),
             pltpu.VMEM(blocks, jnp.bfloat16),
@@ -614,9 +618,9 @@
             pltpu.VMEM((field_count // CHUNKS, bead_count, 2 * cl_wide), jnp.float32),
             pltpu.VMEM((2, 4, field_count, 2 * cl_wide), jnp.float32),
             pltpu.VMEM((2, field_count, 128), jnp.float32),
-            pltpu.VMEM(cluster_waves.shape, jnp.float32),
-            pltpu.VMEM(cluster_waves.shape, jnp.bfloat16),
-            pltpu.VMEM(cluster_waves.shape, jnp.bfloat16),
+            pltpu.VMEM((cl_rows * 2 * lanes, 128), jnp.float32),
+            pltpu.VMEM((2, cl_rows, cl_wide), jnp.bfloat16),
+            pltpu.VMEM((2, cl_rows, cl_wide), jnp.bfloat16),
             pltpu.VMEM((2, field_count, 2 * cl_wide), jnp.float32),
             pltpu.VMEM((2, field_count, 2 * cl_wide), jnp.float32),
             pltpu.VMEM((field_count, 2 * cl_wide), jnp.float32),
@@ -637,23 +641,23 @@
             dma((4,)),
         ],
         compiler_params=pltpu.CompilerParams(
-            collective_id=0, has_side_effects=True, vmem_limit_bytes=40 * 1024 * 1024
+            collective_id=0, has_side_effects=True, vmem_limit_bytes=56 * 1024 * 1024
         ),
         name="krylov",
     )(
-        source,
+        incident[0, 0],
         column_pos,
         row_pos,
         times,
         dirs,
-        forward_matrix,
-        back_matrix,
-        mie_rows,
+        to_waves,
+        jnp.transpose(from_waves, (0, 2, 1)),
+        mie,
         to_cluster,
         cluster_dirs,
-        cluster_waves,
+        flat_waves,
     )
-    expansions = jnp.concatenate([expansion[0], expansion[1]], axis=1)
+    expansions = jnp.concatenate([expansion[0, :, :cl_coef], expansion[1, :, :cl_coef]], axis=1)
     return (jnp.transpose(answer, (1, 0, 2))[None, None], expansions[None])
 
 

time: 98.6 us -> 88.6 us (0.90)
  local copies, waits for them, and re-layouts: 15.8 us -> 4.5 us
  Pallas kernels: 70.2 us -> 73.1 us
  other arithmetic: 10.1 us -> 8.92 us
    unnamed x10 -> x2, local copies, waits for them, and re-layouts: 12.8 us -> 2.82 us
    pallas_call x1, Pallas kernels: 70.2 us -> 73.1 us  [local(): pl.pallas_call(functools.partial(krylov_kernel, nx, ny), out_shape=(jax.S...]
    neg x3 -> x0, other arithmetic: 1.42 us -> none  [the longest x2 0.73 us: block_matrix(): lower_half = jnp.concatenate([-pair[1], pair[0]], axis=1)]
    mul x7 -> x0, local copies, waits for them, and re-layouts: 1.22 us -> none  [the longest x1 0.76 us: times_phase(): real_part * cos_part - imag_part * sin_part]
where the time goes in v4:
time: 88.6 us; the launch traced here: 87.2 us
  Pallas kernels  73.1 us (83%)
  other arithmetic  8.92 us (10%)
  local copies, waits for them, and re-layouts  4.5 us (5%)
    pallas_call x1, Pallas kernels, local(): pl.pallas_call(functools.partial(krylov_kernel, nx, ny), out_shape=(jax.S...  73.1 us
    reduce_sum x1, other arithmetic, local(): jnp.sum((flat_index[:, None, :] == rows[None, :, None]).astype(jnp.float3...  3.1 us
    unnamed x2, local copies, waits for them, and re-layouts  2.82 us

profile of v4, /device:TPU:10, one launch (start us, length us, event | category | flops | bytes accessed | tf_op | source)
XLA Modules:
  0.0 87.2 jit_solution(4496788204956995444)
XLA Ops:
  0.6 0.7 fusion.4
  1.3 0.1 pad.18.clone
  1.4 0.7 copy.35
  2.1 0.7 select_maximum_fusion.row_pos
  2.7 0.7 fusion.1
  3.4 0.8 multiply_reduce_fusion
  4.2 0.7 fusion.5
  4.8 0.1 pad_maximum_fusion
  4.9 0.1 copy.25
  5.0 0.6 pad.8.column_pos
  5.6 0.8 multiply_add_fusion
  6.5 0.7 fusion
  7.1 0.1 pad_add_fusion
  7.2 3.1 %convert_reduce_fusion = f32[576,128]{1,0:T(8,128)} fusion(s32[60,128]{1,0:T(8,128)S(1)} %pad_add_fusion), kind=kLoop, calls=%fused_computation | loop fusion | flops 13197312 | bytes 325632 | tf_op jit(solution)/shard_map/reduce_sum | solution.py:561
  10.3 73.1 %krylov.1 = (f32[16,64,128]{2,1,0:T(8,128)}, f32[2,16,976]{2,1,0:T(8,128)}) custom-call(f32[64,16,128]{2,1,0:T(8,128)} %bitcast.38, f32[64,128]{1,0:T(8,128)} %pad.8.column_pos, f32[8,128]{1,0:T(8,128)} %select_maximum_fusion.row_pos, f32[9,64,128]{2,1,0:T(8,128)} %bitcast.37, f32[8,128]{1,0:T(8,128)} %constant.50.clone.dirs, bf16[2,64,128]{2,1,0:T(8,128)(2,1)} %to_waves.1, ...), custom_call_target="tpu_custom_call" | custom-call | tf_op jit(solution)/shard_map/krylov/pallas_call | solution.py:592
  83.4 2.1 %copy.27 = f32[1,1,64,16,128]{4,3,2,1,0:T(8,128)} copy(f32[1,1,64,16,128]{4,2,3,1,0:T(8,128)} %bitcast.39) | data formatting | bytes 1048576
  85.6 0.9 %slice_bitcast_fusion.1 = (f32[16,961]{1,0:T(8,128)S(1)}, f32[16,961]{1,0:T(8,128)S(1)}) fusion(f32[2,16,976]{2,1,0:T(8,128)} %get-tuple-element.5), kind=kLoop, calls=%fused_computation.4 | loop fusion | bytes 246016 | tf_op jit(solution)/shard_map/squeeze | solution.py:660
  86.5 0.7 maximum_bitcast_fusion
  (2 shorter events, 0.0 us)

commit v5 on v4

--- a/solution.py
+++ b/solution.py
@@ -57,7 +57,7 @@
     return y1 / beta + y2 * p, y2 * r
 
 
-CHUNKS = 2
+CHUNKS = 4
 SHIFTS = [(dx, dy) for dx in (-1, 0, 1) for dy in (-1, 0, 1)]
 
 
@@ -404,8 +404,9 @@
     waves_copy.wait()
 
     lanes = cl_wide // 128
-    for block in range(lanes):
-        for part in range(2):
+
+    def halve(part):
+        for block in range(lanes):
             rows = waves_high.shape[1]
             high, low = split(waves[pl.ds(2 * block + part, rows, stride=2 * lanes), :])
             waves_high[part, :, 128 * block : 128 * block + 128] = high
@@ -428,7 +429,7 @@
 
         gram = loop(c * step, (c + 1) * step, second, gram, 2)
 
-    def reduce_over(gram, slots, send, recv, count, peer):
+    def reduce_over(gram, slots, send, recv, count, peer, part):
         slots[0] = gram
         copies = []
         for d in range(1, count):
@@ -442,6 +443,7 @@
             )
             copy.start()
             copies.append(copy)
+        halve(part)
         for d, copy in enumerate(copies):
             copy.wait_recv()
             gram = gram + slots[d + 1]
@@ -449,8 +451,8 @@
             copy.wait_send()
         return gram
 
-    gram = reduce_over(gram, gram_x, x_send, x_recv, nx, lambda d: (lax.rem(i + d, nx), j))
-    gram = reduce_over(gram, gram_y, y_send, y_recv, ny, lambda d: (i, lax.rem(j + d, ny)))
+    gram = reduce_over(gram, gram_x, x_send, x_recv, nx, lambda d: (lax.rem(i + d, nx), j), 0)
+    gram = reduce_over(gram, gram_y, y_send, y_recv, ny, lambda d: (i, lax.rem(j + d, ny)), 1)
     w_source, w_once = weights([gram[k : k + 1] for k in range(6)])
     diagonal = lax.broadcasted_iota(jnp.int32, (fields, 128), 0) == lax.broadcasted_iota(
         jnp.int32, (fields, 128), 1

time: 88.6 us -> 85.4 us (0.964)
  Pallas kernels: 73.1 us -> 70.4 us
    pallas_call x1, Pallas kernels: 73.1 us -> 70.4 us  [local(): pl.pallas_call(functools.partial(krylov_kernel, nx, ny), out_shape=(jax.S...]
where the time goes in v5:
time: 85.4 us; the launch traced here: 84.5 us
  Pallas kernels  70.4 us (82%)
  other arithmetic  8.92 us (10%)
  local copies, waits for them, and re-layouts  4.5 us (5%)
    pallas_call x1, Pallas kernels, local(): pl.pallas_call(functools.partial(krylov_kernel, nx, ny), out_shape=(jax.S...  70.4 us
    reduce_sum x1, other arithmetic, local(): jnp.sum((flat_index[:, None, :] == rows[None, :, None]).astype(jnp.float3...  3.1 us
    unnamed x2, local copies, waits for them, and re-layouts  2.82 us

profile of v5, /device:TPU:10, one launch (start us, length us, event | category | flops | bytes accessed | tf_op | source)
XLA Modules:
  0.0 84.5 jit_solution(2567333049935828668)
XLA Ops:
  0.6 0.7 fusion.4
  1.3 0.1 pad.18.clone
  1.4 0.7 copy.35
  2.1 0.7 select_maximum_fusion.row_pos
  2.7 0.7 fusion.1
  3.4 0.8 multiply_reduce_fusion
  4.2 0.7 fusion.5
  4.8 0.1 pad_maximum_fusion
  4.9 0.1 copy.25
  5.0 0.6 pad.8.column_pos
  5.6 0.8 multiply_add_fusion
  6.5 0.7 fusion
  7.1 0.1 pad_add_fusion
  7.2 3.1 %convert_reduce_fusion = f32[576,128]{1,0:T(8,128)} fusion(s32[60,128]{1,0:T(8,128)S(1)} %pad_add_fusion), kind=kLoop, calls=%fused_computation | loop fusion | flops 13197312 | bytes 325632 | tf_op jit(solution)/shard_map/reduce_sum | solution.py:563
  10.3 70.4 %krylov.1 = (f32[16,64,128]{2,1,0:T(8,128)}, f32[2,16,976]{2,1,0:T(8,128)}) custom-call(f32[64,16,128]{2,1,0:T(8,128)} %bitcast.38, f32[64,128]{1,0:T(8,128)} %pad.8.column_pos, f32[8,128]{1,0:T(8,128)} %select_maximum_fusion.row_pos, f32[9,64,128]{2,1,0:T(8,128)} %bitcast.37, f32[8,128]{1,0:T(8,128)} %constant.50.clone.dirs, bf16[2,64,128]{2,1,0:T(8,128)(2,1)} %to_waves.1, ...), custom_call_target="tpu_custom_call" | custom-call | tf_op jit(solution)/shard_map/krylov/pallas_call | solution.py:594
  80.7 2.1 %copy.27 = f32[1,1,64,16,128]{4,3,2,1,0:T(8,128)} copy(f32[1,1,64,16,128]{4,2,3,1,0:T(8,128)} %bitcast.39) | data formatting | bytes 1048576
  82.8 0.9 %slice_bitcast_fusion.1 = (f32[16,961]{1,0:T(8,128)S(1)}, f32[16,961]{1,0:T(8,128)S(1)}) fusion(f32[2,16,976]{2,1,0:T(8,128)} %get-tuple-element.5), kind=kLoop, calls=%fused_computation.4 | loop fusion | bytes 246016 | tf_op jit(solution)/shard_map/squeeze | solution.py:662
  83.7 0.7 maximum_bitcast_fusion
  (2 shorter events, 0.0 us)
